TPU v7x, 256 devices: a whole 4x4x8 slice. The times are simulated.
256 devices in a mesh: wide: 32 (over x_lo, z, core), narrow: 8 (over x_hi, y).
Axes of the slice: x: 4 (x_hi: 2, x_lo: 2; x = x_hi * 2 + x_lo), y: 4, z: 8, core: 2. Of those that a mesh axis runs over, the one named last changes fastest.
Arguments:
- points: bfloat16 [65536, 1024], P(('wide', 'narrow')), may hold values from -6 to 6
- seg_lengths: int32 [256, 32], P(('wide', 'narrow')), may hold values from 1 to 128, 256 in all within a row
- seg_owner: int32 [256, 32, 1], P(('wide', 'narrow')), may hold values from 0 to 7; in each aligned block of 32 rows (0 to 31, 32 to 63, ..., all dimensions but the last counted through in order) at most 8 rows name the same one
- seg_row: int32 [256, 32], P(('wide', 'narrow')), may hold values from 0 to 1535
- level_two: bfloat16 [131072, 1024], P('wide'), may hold values from -6 to 6
Outputs:
- means: float32 [12288, 1024], P('narrow', 'wide')
- scores: bfloat16 [12288, 131072], P('narrow', 'wide')
Inputs may be any that keep to these rules, and one draw needn't show every extreme that they name: `seg_lengths`: each device's 32 lengths sum to 256; in every device's row one length equals 128. `seg_owner`: among the 32 runs of one device, at most 8 name the same owner; some device's runs name one owner exactly 8 times.
All inputs are finite; a program needn't handle non-finite values.
Results may differ from a plain program's by a relative error of at most 0.0049.
Values may be sent and summed in bfloat16 or wider, within the bound.
No kernel may reach another device: no remote copies, remote signals or barrier semaphores. Data moves between devices by JAX's collectives and lax.ppermute only.
A program may use at most 128 MiB of HBM per device.

v0:
```python
import jax
import jax.numpy as jnp
from jax import lax
from jax.sharding import PartitionSpec as P

K1S = 1536


def place_rows(row_ids, sums, counts):
    row_hot = (row_ids[None, :] == lax.iota(jnp.int32, K1S).astype(jnp.float32)[:, None]).astype(
        jnp.float32
    )
    placed = jnp.dot(row_hot, sums, precision=lax.Precision.HIGHEST)
    placed_counts = jnp.dot(row_hot, counts, precision=lax.Precision.HIGHEST)
    return (placed, placed_counts)


def local(points, seg_lengths, seg_owner, seg_row, level_two):
    narrow = lax.axis_size("narrow")
    wide = lax.axis_size("wide")
    lengths = seg_lengths[0]
    owners = seg_owner[0, :, 0]
    centre_rows = seg_row[0]
    segments = lengths.shape[0]
    capacity = segments * 2 // narrow
    width = points.shape[1]
    ends = jnp.cumsum(lengths)
    starts = ends - lengths
    position = lax.iota(jnp.int32, points.shape[0])
    member = ((position[None, :] >= starts[:, None]) & (position[None, :] < ends[:, None])).astype(
        jnp.bfloat16
    )
    run_sums = jnp.dot(member, points, preferred_element_type=jnp.float32)
    owner_hot = (owners[:, None] == lax.iota(jnp.int32, narrow)[None, :]).astype(jnp.int32)
    ranking = jnp.cumsum(owner_hot, axis=0) - 1
    run_rank = jnp.sum(ranking * owner_hot, axis=1)
    slot_index = owners * capacity + run_rank
    placing = (slot_index[:, None] == lax.iota(jnp.int32, narrow * capacity)[None, :]).astype(
        jnp.float32
    )
    send_sums = jnp.dot(placing.T, run_sums, precision=lax.Precision.HIGHEST).reshape(
        narrow, capacity, width
    )
    send_counts = jnp.dot(
        placing.T, lengths.astype(jnp.float32), precision=lax.Precision.HIGHEST
    ).reshape(narrow, capacity)
    send_rows = jnp.dot(
        placing.T, centre_rows.astype(jnp.float32), precision=lax.Precision.HIGHEST
    ).reshape(narrow, capacity)
    recv_sums, recv_counts, recv_rows = (
        lax.all_to_all(send_sums, "narrow", split_axis=0, concat_axis=0, tiled=True),
        lax.all_to_all(send_counts, "narrow", split_axis=0, concat_axis=0, tiled=True),
        lax.all_to_all(send_rows, "narrow", split_axis=0, concat_axis=0, tiled=True),
    )
    recv_sums = recv_sums.reshape(narrow * capacity, width)
    recv_counts = recv_counts.reshape(narrow * capacity)
    recv_rows = recv_rows.reshape(narrow * capacity)
    share_width = width // wide
    partial_value, partial_counts = place_rows(recv_rows, recv_sums, recv_counts)
    totals, tally = lax.psum((partial_value, partial_counts), "wide")
    own_part = lax.dynamic_slice_in_dim(
        totals, lax.axis_index("wide") * share_width, share_width, 1
    )
    means = own_part / jnp.maximum(tally, 1.0)[:, None]
    unit = (totals / jnp.sqrt(jnp.sum(totals * totals, axis=1) + 1e-06)[:, None]).astype(
        jnp.bfloat16
    )
    scores = lax.dot_general(
        unit, level_two, (((1,), (1,)), ((), ())), preferred_element_type=jnp.float32
    )
    return (means, scores.astype(jnp.bfloat16))


def solution(mesh):
    return jax.shard_map(
        local,
        mesh=mesh,
        in_specs=(
            P(("wide", "narrow"), None),
            P(("wide", "narrow"), None),
            P(("wide", "narrow"), None, None),
            P(("wide", "narrow"), None),
            P("wide", None),
        ),
        out_specs=(P("narrow", "wide"), P("narrow", "wide")),
        check_vma=False,
    )
```

profile of v0, /device:TPU:1, one launch (start us, length us, event | category | flops | bytes accessed | tf_op | source)
XLA Modules:
  0.0 316.8 jit_solution(10545788497686870075)
XLA Ops:
  7.2 0.0 copy-start
  7.2 0.8 fusion.20
  8.0 0.1 reduce_window_sum.18
  8.0 0.8 select_reduce_fusion
  8.9 0.7 multiply_add_fusion.1
  9.5 1.6 convolution_bitcast_fusion.2
  11.2 7.5 %all-to-all-start = ((f32[8,1,8]{2,1,0:T(1,128)}), f32[8,1,8]{2,1,0:T(1,128)S(1)}, u32[]{:S(2)}, u32[]{:S(2)}) async-start(f32[8,1,8]{2,1,0:T(1,128)} %convolution_bitcast_fusion.2), calls=%async_computation | async-start | bytes 8192 | tf_op jit(solution)/shard_map/all_to_all | solution.py:53
  18.7 0.7 copy.12
  19.4 0.1 reduce-window.7
  19.5 0.1 reduce.1
  19.6 0.7 bitcast_subtract_fusion
  20.2 0.0 copy-done
  20.2 0.2 fusion.12
  20.5 1.1 convolution_bitcast_fusion
  21.6 3.5 %all-to-all-done = f32[8,1,8]{2,1,0:T(1,128)S(1)} async-done(((f32[8,1,8]{2,1,0:T(1,128)}), f32[8,1,8]{2,1,0:T(1,128)S(1)}, u32[]{:S(2)}, u32[]{:S(2)}) %all-to-all-start) | async-done | bytes 288 | tf_op jit(solution)/shard_map/all_to_all | solution.py:53
  25.1 3.4 %all-to-all-start.1 = ((f32[8,8,1024]{2,1,0:T(8,128)}), f32[8,8,1024]{2,1,0:T(8,128)S(1)}, u32[]{:S(2)}, u32[]{:S(2)}) async-start(f32[8,8,1024]{2,1,0:T(8,128)} %convolution_bitcast_fusion), calls=%async_computation.1 | async-start | bytes 524288 | tf_op jit(solution)/shard_map/all_to_all | solution.py:51
  28.5 0.0 all-reduce.2.cloned.1.call-start
  28.6 0.5 broadcast.56
  29.1 0.6 reduce.9
  29.7 0.1 eq.70
  29.8 0.0 copy-start.1
  29.8 6.4 %all-to-all-done.1 = f32[8,8,1024]{2,1,0:T(8,128)S(1)} async-done(((f32[8,8,1024]{2,1,0:T(8,128)}), f32[8,8,1024]{2,1,0:T(8,128)S(1)}, u32[]{:S(2)}, u32[]{:S(2)}) %all-to-all-start.1) | async-done | bytes 262176 | tf_op jit(solution)/shard_map/all_to_all | solution.py:51
  36.2 4.7 %fusion.2 = f32[1536,1024]{1,0:T(8,128)} fusion(f32[64]{0:T(128)S(1)} %eq.70, f32[1536]{0:T(1024)S(1)} %iota_convert_fusion, f32[8,8,1024]{2,1,0:T(8,128)S(1)} %all-to-all-done.1), kind=kOutput, calls=%fused_computation.9 | convolution fusion | flops 1208057856 | bytes 6560000 | tf_op jit(solution)/shard_map/dot_general | solution.py:13
  40.9 0.0 all-reduce.2.cloned.1.call-update
  41.0 0.0 copy-done.1
  41.0 1.0 convolution_bitcast_fusion.1
  42.0 3.3 %all-to-all-start.2 = ((f32[8,1,8]{2,1,0:T(1,128)}), f32[8,1,8]{2,1,0:T(1,128)S(1)}, u32[]{:S(2)}, u32[]{:S(2)}) async-start(f32[8,1,8]{2,1,0:T(1,128)} %convolution_bitcast_fusion.1), calls=%async_computation.2 | async-start | bytes 8192 | tf_op jit(solution)/shard_map/all_to_all | solution.py:52
  45.3 6.4 %all-to-all-done.2 = f32[8,1,8]{2,1,0:T(1,128)S(1)} async-done(((f32[8,1,8]{2,1,0:T(1,128)}), f32[8,1,8]{2,1,0:T(1,128)S(1)}, u32[]{:S(2)}, u32[]{:S(2)}) %all-to-all-start.2) | async-done | bytes 288 | tf_op jit(solution)/shard_map/all_to_all | solution.py:52
  51.6 0.6 reduce.10
  52.2 0.1 reshape.108
  52.3 0.6 convolution_reduce_fusion
  52.9 59.7 %psum.15 = f32[1536]{0:T(1024)S(1)} all-reduce(f32[1536]{0:T(1024)S(1)} %convolution_reduce_fusion), channel_id=1, replica_groups=mesh['wide'=32,'narrow'=8] {'wide'}, use_global_device_ids=true, to_apply=%region_4.5 | all-reduce | flops 1536 | bytes 12288 | tf_op jit(solution)/shard_map/psum | solution.py:60
  112.7 170.7 %all-reduce.2.cloned.1.call-done = f32[1536,1024]{1,0:T(8,128)} async-done(((f32[1536,1024]{1,0:T(8,128)}), f32[1536,1024]{1,0:T(8,128)}) %all-reduce.2.cloned.1.call-update) | async-done | bytes 6291472 | tf_op jit(solution)/shard_map/psum | solution.py:60
  283.4 3.3 %multiply_reduce_fusion = f32[1536]{0:T(1024)S(1)} fusion(f32[1536,1024]{1,0:T(8,128)} %all-reduce.2.cloned.1.call-done), kind=kLoop, calls=%fused_computation.2 | loop fusion | flops 3144192 | bytes 6297600 | tf_op jit(solution)/shard_map/reduce_sum | solution.py:65
  286.7 1.6 dynamic-slice_divide_fusion
  288.3 0.9 copy.14
  289.2 20.7 %convolution_convert_fusion = bf16[1536,4096]{1,0:T(8,128)(2,1)} fusion(bf16[4096,1024]{1,0:T(8,128)(2,1)} %param.9, f32[1536,1024]{1,0:T(8,128)} %all-reduce.2.cloned.1.call-done, f32[1536]{0:T(1024)S(1)} %add_sqrt_fusion), kind=kOutput, calls=%fused_computation | convolution fusion | flops 12894339072 | bytes 27269120 | tf_op jit(solution)/shard_map/dot_general | solution.py:68
  (4 shorter events, 0.0 us)
Async XLA Ops:
  7.2 13.1 %copy-start = (bf16[256,1024]{1,0:T(8,128)(2,1)S(1)}, bf16[256,1024]{1,0:T(8,128)(2,1)}, u32[]{:S(2)}) copy-start(bf16[256,1024]{1,0:T(8,128)(2,1)} %param.5) | copy-start | bytes 1572868
  11.2 13.9 %all-to-all-start = ((f32[8,1,8]{2,1,0:T(1,128)}), f32[8,1,8]{2,1,0:T(1,128)S(1)}, u32[]{:S(2)}, u32[]{:S(2)}) async-start(f32[8,1,8]{2,1,0:T(1,128)} %convolution_bitcast_fusion.2), calls=%async_computation | async-start | bytes 8192 | tf_op jit(solution)/shard_map/all_to_all | solution.py:53
  25.1 11.1 %all-to-all-start.1 = ((f32[8,8,1024]{2,1,0:T(8,128)}), f32[8,8,1024]{2,1,0:T(8,128)S(1)}, u32[]{:S(2)}, u32[]{:S(2)}) async-start(f32[8,8,1024]{2,1,0:T(8,128)} %convolution_bitcast_fusion), calls=%async_computation.1 | async-start | bytes 524288 | tf_op jit(solution)/shard_map/all_to_all | solution.py:51
  28.5 254.9 %all-reduce.2.cloned.1.call-start = ((), (), s32[]{:S(2)}) async-start(), calls=%async_computation.3 | async-start | bytes 12582912 | tf_op jit(solution)/shard_map/psum | solution.py:60
  29.8 11.2 %copy-start.1 = (s32[1,32]{1,0:T(1,128)S(1)}, s32[1,32]{1,0:T(1,128)}, u32[]{:S(2)}) copy-start(s32[1,32]{1,0:T(1,128)} %param.6) | copy-start | bytes 388
  42.0 9.7 %all-to-all-start.2 = ((f32[8,1,8]{2,1,0:T(1,128)}), f32[8,1,8]{2,1,0:T(1,128)S(1)}, u32[]{:S(2)}, u32[]{:S(2)}) async-start(f32[8,1,8]{2,1,0:T(1,128)} %convolution_bitcast_fusion.1), calls=%async_computation.2 | async-start | bytes 8192 | tf_op jit(solution)/shard_map/all_to_all | solution.py:52
Sparse Core Ops, SparseCore 0:
  41.1 242.2 all-reduce.1
where the time goes:
time: 317 us
  waiting for transfers between devices  187 us (59%)
  blocking collectives  59.7 us (19%)
  matrix products  30 us (9%)
  starting transfers between devices  14.2 us (4%)
  between operations  14.1 us (4%)
  other arithmetic  9.24 us (3%)
    psum x1, waiting for transfers between devices, local(): totals, tally = lax.psum((partial_value, partial_counts), 'wide')  171 us
    psum x1, blocking collectives, local(): totals, tally = lax.psum((partial_value, partial_counts), 'wide')  59.7 us
    dot_general x1, matrix products, local(): lax.dot_general(unit, level_two, (((1,), (1,)), ((), ())), preferred_elem...  20.7 us
    all_to_all x1, starting transfers between devices, local(): lax.all_to_all(send_rows, 'narrow', split_axis=0, concat_axis=0, tiled=True)  7.48 us
    all_to_all x1, waiting for transfers between devices, local(): lax.all_to_all(send_sums, 'narrow', split_axis=0, concat_axis=0, tiled=True)  6.42 us
    all_to_all x1, waiting for transfers between devices, local(): lax.all_to_all(send_counts, 'narrow', split_axis=0, concat_axis=0, tiled=...  6.36 us
  transfers between devices with their start and end apart: 4, of which 4 were waited for; matrix products, arithmetic and copies ran while one was open for 2% of the time, Pallas kernels for 0%

commit v1 on v0

v1 whole, which is shorter than its diff:
```python
import jax
import jax.numpy as jnp
from jax import lax
from jax.experimental import pallas as pl
from jax.experimental.pallas import tpu as pltpu
from jax.sharding import PartitionSpec as P

K1S = 1536
K2S = 4096
D = 1024
HALF = 512
SEGS = 32
CAP = 8
NARROW = 8
SLOTS = 256
BLOCK = 272
LANES = 128
F32 = jnp.float32
BF16 = jnp.bfloat16

ALL = ("wide", "narrow")


def wide_of(x, z, c):
    return (x * 8 + z % 8) * 2 + c


WIDES = [(x, z, c) for x in range(2) for z in range(8) for c in range(2)]
PLANES = [
    [wide_of(x, z, c) * NARROW + n for x in range(2) for c in range(2) for n in range(NARROW)]
    for z in range(8)
]
CORE_SWAP = [(wide_of(x, z, c), wide_of(x, z, 1 - c)) for x, z, c in WIDES]


def z_shift(step):
    return [(wide_of(x, z, c), wide_of(x, z + step, c)) for x, z, c in WIDES]


def iota2(shape, axis):
    return lax.broadcasted_iota(jnp.int32, shape, axis)


def pack_kernel(points_ref, lengths_ref, owner_ref, rows_ref, out_ref):
    r, q = iota2((SEGS, SEGS), 0), iota2((SEGS, SEGS), 1)
    eye = (r == q).astype(F32)
    length_row = lengths_ref[...].astype(F32)
    id_row = rows_ref[...].astype(F32)
    length = jnp.sum(eye * length_row, axis=1, keepdims=True)
    ends = jnp.sum(jnp.where(q <= r, length_row, 0.0), axis=1, keepdims=True)
    ids = jnp.sum(eye * id_row, axis=1, keepdims=True)
    position = iota2((SEGS, 256), 1).astype(F32)
    member = ((position >= ends - length) & (position < ends)).astype(BF16)
    runs = jnp.dot(member, points_ref[...], preferred_element_type=F32).astype(BF16)

    owner = owner_ref[0].astype(F32)
    owner_row = jnp.sum(eye * owner, axis=0, keepdims=True)
    rank_row = jnp.sum(jnp.where((owner == owner_row) & (r < q), 1.0, 0.0), axis=0, keepdims=True)
    slot_row = owner_row * CAP + rank_row
    place = (iota2((NARROW * CAP, SEGS), 0).astype(F32) == slot_row).astype(BF16)
    slots = jnp.dot(place, runs, preferred_element_type=F32).astype(BF16)
    high = jnp.floor(ids * (1.0 / 16.0))
    low = ids - 16.0 * high
    lane = iota2((SEGS, LANES), 1)
    tags = jnp.where(lane == 0, high, jnp.where(lane == 1, low, jnp.where(lane == 2, length, 0.0)))
    tags = jnp.dot(place, tags.astype(BF16), preferred_element_type=F32).astype(BF16)
    per = NARROW * CAP
    for x in range(2):
        for c in range(2):
            at = pl.ds((x * 2 + c) * per, per)
            out_ref[at, :HALF] = slots[:, c * HALF : (c + 1) * HALF]
            out_ref[at, HALF:] = tags


def block_kernel(received_ref, out_ref):
    out_ref[:SLOTS, :] = received_ref[:, :HALF]
    tags = received_ref[:, HALF:].astype(F32)
    turned = jnp.concatenate([tags[:LANES].T[:16], tags[LANES:].T[:16]], axis=1)
    out_ref[SLOTS:, :SLOTS] = turned.astype(BF16)
    out_ref[SLOTS:, SLOTS:] = jnp.zeros((16, HALF - SLOTS), BF16)


CHUNK = 256


def place_kernel(*refs):
    blocks, sums_ref, counts_ref = refs[:-2], refs[-2], refs[-1]

    @pl.loop(0, K1S // CHUNK)
    def _(i):
        row = (iota2((CHUNK, SLOTS), 0) + i * CHUNK).astype(F32)
        total = jnp.zeros((CHUNK, HALF), F32)
        tally = jnp.zeros((CHUNK, 16), F32)
        for ref in blocks:
            tags = ref[SLOTS:, :SLOTS]
            ids = tags[0:1].astype(F32) * 16.0 + tags[1:2].astype(F32)
            hot = (row == ids).astype(BF16)
            total += jnp.dot(hot, ref[:SLOTS, :], preferred_element_type=F32)
            tally += lax.dot_general(hot, tags, (((1,), (1,)), ((), ())), preferred_element_type=F32)
        at = pl.ds(pl.multiple_of(i * CHUNK, CHUNK), CHUNK)
        sums_ref[at, :] = total.astype(BF16)
        counts_ref[at, :] = tally


TILE = 512


def score_kernel(own_ref, other_ref, counts_ref, two_ref, means_ref, scores_ref, sums, inverse):
    w = lax.axis_index("wide")
    core = w % 2

    @pl.when(pl.program_id(0) == 0)
    def _():
        sums[:, pl.ds(pl.multiple_of(core * HALF, HALF), HALF)] = own_ref[...]
        sums[:, pl.ds(pl.multiple_of((1 - core) * HALF, HALF), HALF)] = other_ref[...]

        @pl.loop(0, K1S // CHUNK)
        def _(i):
            at = pl.ds(pl.multiple_of(i * CHUNK, CHUNK), CHUNK)
            part = sums[at, :].astype(F32)
            square = jnp.sum(part * part, axis=1, keepdims=True)
            inverse[at, :] = jnp.broadcast_to(1.0 / jnp.sqrt(square + 1e-06), (CHUNK, LANES))
            lanes = pl.ds(pl.multiple_of(w // 4 * LANES, LANES), LANES)
            mine = pltpu.roll(sums[at, lanes].astype(F32), (4 - w % 4) % 4 * 32, 1)[:, :32]
            means_ref[at, :] = mine / jnp.maximum(counts_ref[at, 2:3], 1.0)

    @pl.loop(0, K1S // CHUNK)
    def _(i):
        at = pl.ds(pl.multiple_of(i * CHUNK, CHUNK), CHUNK)
        product = lax.dot_general(
            sums[at, :], two_ref[...], (((1,), (1,)), ((), ())), preferred_element_type=F32
        )
        scores_ref[at, :] = (product * inverse[at, 0:1]).astype(BF16)


def whole(shape):
    return pl.BlockSpec(shape, lambda *_: (0,) * len(shape))


def local(points, seg_lengths, seg_owner, seg_row, level_two):
    vmem = pl.BlockSpec(memory_space=pltpu.VMEM)
    send = pl.pallas_call(
        pack_kernel,
        out_shape=jax.ShapeDtypeStruct((SLOTS, HALF + LANES), BF16),
        in_specs=[vmem] * 4,
        out_specs=vmem,
        name="pack",
    )(points, seg_lengths, seg_owner, seg_row)
    received = lax.all_to_all(send, ALL, 0, 0, axis_index_groups=PLANES, tiled=True)
    block = pl.pallas_call(
        block_kernel,
        out_shape=jax.ShapeDtypeStruct((BLOCK, HALF), BF16),
        in_specs=[vmem],
        out_specs=vmem,
        name="block",
    )(received)

    up = down = block
    blocks = [block]
    for _ in range(3):
        up = lax.ppermute(up, "wide", z_shift(1))
        down = lax.ppermute(down, "wide", z_shift(-1))
        blocks += [up, down]
    last = lax.ppermute(up, "wide", z_shift(1))
    blocks.append(last)

    sums, counts = pl.pallas_call(
        place_kernel,
        out_shape=(jax.ShapeDtypeStruct((K1S, HALF), BF16), jax.ShapeDtypeStruct((K1S, 16), F32)),
        in_specs=[vmem] * len(blocks),
        out_specs=(vmem, vmem),
        compiler_params=pltpu.CompilerParams(vmem_limit_bytes=40 << 20),
        name="place",
    )(*blocks)
    other = lax.ppermute(sums, "wide", CORE_SWAP)

    means, scores = pl.pallas_call(
        score_kernel,
        grid=(K2S // TILE,),
        out_shape=(jax.ShapeDtypeStruct((K1S, 32), F32), jax.ShapeDtypeStruct((K1S, K2S), BF16)),
        in_specs=[
            whole((K1S, HALF)),
            whole((K1S, HALF)),
            whole((K1S, 16)),
            pl.BlockSpec((TILE, D), lambda j: (j, 0)),
        ],
        out_specs=(whole((K1S, 32)), pl.BlockSpec((K1S, TILE), lambda j: (0, j))),
        scratch_shapes=[pltpu.VMEM((K1S, D), BF16), pltpu.VMEM((K1S, LANES), F32)],
        compiler_params=pltpu.CompilerParams(vmem_limit_bytes=48 << 20),
        name="score",
    )(sums, other, counts, level_two)
    return means, scores


def solution(mesh):
    return jax.shard_map(
        local,
        mesh=mesh,
        in_specs=(
            P(ALL, None),
            P(ALL, None),
            P(ALL, None, None),
            P(ALL, None),
            P("wide", None),
        ),
        out_specs=(P("narrow", "wide"), P("narrow", "wide")),
        check_vma=False,
    )
```

time: 317 us -> 99.6 us (0.31)
  waiting for transfers between devices: 187 us -> 23.8 us
  blocking collectives: 59.7 us -> 17.5 us
  Pallas kernels: 0 us -> 36.8 us
  matrix products: 30 us -> 0 us
  between operations: 14.1 us -> 0.65 us
  other arithmetic: 9.24 us -> 0 us
    psum x1 -> x0, waiting for transfers between devices: 171 us -> none  [local(): totals, tally = lax.psum((partial_value, partial_counts), 'wide')]
    psum x1 -> x0, blocking collectives: 59.7 us -> none  [local(): totals, tally = lax.psum((partial_value, partial_counts), 'wide')]
    pallas_call x0 -> x4, Pallas kernels: none -> 36.8 us  [the longest x1 27 us: local(): pl.pallas_call(score_kernel, grid=(K2S // TILE,), out_shape=(jax.ShapeDty...]
    dot_general x7 -> x0, matrix products: 30 us -> none  [the longest x1 20.7 us: local(): lax.dot_general(unit, level_two, (((1,), (1,)), ((), ())), preferred_elem...]
    ppermute x0 -> x8, waiting for transfers between devices: none -> 23.8 us  [the longest x3 14.2 us: local(): up = lax.ppermute(up, 'wide', z_shift(1))]
    all_to_all x0 -> x1, blocking collectives: none -> 17.5 us  [local(): lax.all_to_all(send, ALL, 0, 0, axis_index_groups=PLANES, tiled=True)]
    ppermute x0 -> x8, starting transfers between devices: none -> 16.4 us  [the longest x3 9.29 us: local(): down = lax.ppermute(down, 'wide', z_shift(-1))]
    all_to_all x3 -> x0, waiting for transfers between devices: 16.3 us -> none  [the longest x1 6.42 us: local(): lax.all_to_all(send_sums, 'narrow', split_axis=0, concat_axis=0, tiled=True)]
  transfers between devices with their start and end apart: 4 -> 8, of which waited for: 4 -> 5; matrix products, arithmetic and copies ran while one was open for 2% -> 0% of each run, Pallas kernels for 0% -> 0%
where the time goes in v1:
time: 99.6 us; the launch traced here: 98.4 us
  Pallas kernels  36.8 us (37%)
  waiting for transfers between devices  23.8 us (24%)
  blocking collectives  17.5 us (18%)
  starting transfers between devices  16.4 us (16%)
  local copies, waits for them, and re-layouts  3.22 us (3%)
    pallas_call x1, Pallas kernels, local(): pl.pallas_call(score_kernel, grid=(K2S // TILE,), out_shape=(jax.ShapeDty...  27 us
    all_to_all x1, blocking collectives, local(): lax.all_to_all(send, ALL, 0, 0, axis_index_groups=PLANES, tiled=True)  17.5 us
    ppermute x3, waiting for transfers between devices, local(): up = lax.ppermute(up, 'wide', z_shift(1))  14.2 us
    ppermute x3, starting transfers between devices, local(): down = lax.ppermute(down, 'wide', z_shift(-1))  9.29 us
    ppermute x1, waiting for transfers between devices, local(): last = lax.ppermute(up, 'wide', z_shift(1))  6.6 us
    pallas_call x1, Pallas kernels, local(): pl.pallas_call(place_kernel, out_shape=(jax.ShapeDtypeStruct((K1S, HALF),...  5.8 us
    ppermute x1, starting transfers between devices, local(): other = lax.ppermute(sums, 'wide', CORE_SWAP)  5.43 us
    ppermute x1, waiting for transfers between devices, local(): other = lax.ppermute(sums, 'wide', CORE_SWAP)  3.04 us
  transfers between devices with their start and end apart: 8, of which 5 were waited for; matrix products, arithmetic and copies ran while one was open for 0% of the time, Pallas kernels for 0%

profile of v1, /device:TPU:1, one launch (start us, length us, event | category | flops | bytes accessed | tf_op | source)
XLA Modules:
  0.0 98.4 jit_solution(2240908216979894591)
XLA Ops:
  0.6 1.3 %copy.7.owner_ref = s32[1,32,1]{2,1,0:T(8,128)} copy(s32[1,32,1]{1,2,0:T(1,128)} %param.7) | data formatting | bytes 256 | tf_op args[2]
  2.0 2.2 %pack.1 = bf16[256,640]{1,0:T(8,128)(2,1)} custom-call(bf16[256,1024]{1,0:T(8,128)(2,1)} %points_ref.1, s32[1,32]{1,0:T(1,128)} %lengths_ref.1, s32[1,32,1]{2,1,0:T(8,128)} %copy.7.owner_ref, s32[1,32]{1,0:T(1,128)} %rows_ref.1), custom_call_target="tpu_custom_call" | custom-call | tf_op jit(solution)/shard_map/pack/pallas_call | solution.py:142
  4.2 17.5 %all_to_all.11 = bf16[32,8,640]{2,1,0:T(8,128)(2,1)} all-to-all(bf16[32,8,640]{2,1,0:T(8,128)(2,1)} %bitcast.2), channel_id=1, replica_groups={{0,1,2,3,4,5,6,7,8,9,10,11,12,13,14,15,128,129,130,131,132,133,134,135,..., dimensions={0} | all-to-all | bytes 655360 | tf_op jit(solution)/shard_map/all_to_all | solution.py:149
  21.7 1.8 %block.1.refs_0_ = bf16[272,512]{1,0:T(8,128)(2,1)} custom-call(bf16[256,640]{1,0:T(8,128)(2,1)} %bitcast.3), custom_call_target="tpu_custom_call" | custom-call | tf_op jit(solution)/shard_map/block/pallas_call | solution.py:150
  23.5 1.6 %collective-permute-start = (bf16[272,512]{1,0:T(8,128)(2,1)}, bf16[272,512]{1,0:T(8,128)(2,1)S(1)}, u32[]{:S(2)}, u32[]{:S(2)}) collective-permute-start(bf16[272,512]{1,0:T(8,128)(2,1)} %block.1.refs_0_), channel_id=1, source_target_pairs={{0,16},{8,24},{16,32},{24,40},{32,48},{40,56},{48,64},{56,72},{64,... | collective-permute-start | bytes 835592 | tf_op jit(solution)/shard_map/ppermute | solution.py:161
  25.1 3.9 %collective-permute-start.1 = (bf16[272,512]{1,0:T(8,128)(2,1)}, bf16[272,512]{1,0:T(8,128)(2,1)S(1)}, u32[]{:S(2)}, u32[]{:S(2)}) collective-permute-start(bf16[272,512]{1,0:T(8,128)(2,1)} %block.1.refs_0_), channel_id=1, source_target_pairs={{0,112},{8,120},{16,0},{24,8},{32,16},{40,24},{48,32},{56,40},{64,... | collective-permute-start | bytes 835592 | tf_op jit(solution)/shard_map/ppermute | solution.py:162
  29.0 5.7 %collective-permute-done.refs_1_ = bf16[272,512]{1,0:T(8,128)(2,1)S(1)} collective-permute-done((bf16[272,512]{1,0:T(8,128)(2,1)}, bf16[272,512]{1,0:T(8,128)(2,1)S(1)}, u32[]{:S(2)}, u32[]{:S(2)}) %collective-permute-start) | collective-permute-done | bytes 278560 | tf_op jit(solution)/shard_map/ppermute | solution.py:161
  34.7 0.0 collective-permute-start.2
  34.7 0.0 collective-permute-done.1.refs_2_
  34.7 2.7 %collective-permute-start.3 = (bf16[272,512]{1,0:T(8,128)(2,1)S(1)}, bf16[272,512]{1,0:T(8,128)(2,1)S(1)}, u32[]{:S(2)}, u32[]{:S(2)}) collective-permute-start(bf16[272,512]{1,0:T(8,128)(2,1)S(1)} %collective-permute-done.1.refs_2_), channel_id=1, source_target_pairs={{0,112},{8,120},{16,0},{24,8},{32,16},{40,24},{48,32},{56,40},{64,... | collective-permute-start | bytes 835592 | tf_op jit(solution)/shard_map/ppermute | solution.py:162
  37.4 4.6 %collective-permute-done.2.refs_3_ = bf16[272,512]{1,0:T(8,128)(2,1)S(1)} collective-permute-done((bf16[272,512]{1,0:T(8,128)(2,1)S(1)}, bf16[272,512]{1,0:T(8,128)(2,1)S(1)}, u32[]{:S(2)}, u32[]{:S(2)}) %collective-permute-start.2) | collective-permute-done | bytes 278560 | tf_op jit(solution)/shard_map/ppermute | solution.py:161
  42.0 0.0 collective-permute-start.4
  42.0 0.0 collective-permute-done.3.refs_4_
  42.0 2.7 %collective-permute-start.5 = (bf16[272,512]{1,0:T(8,128)(2,1)S(1)}, bf16[272,512]{1,0:T(8,128)(2,1)S(1)}, u32[]{:S(2)}, u32[]{:S(2)}) collective-permute-start(bf16[272,512]{1,0:T(8,128)(2,1)S(1)} %collective-permute-done.3.refs_4_), channel_id=1, source_target_pairs={{0,112},{8,120},{16,0},{24,8},{32,16},{40,24},{48,32},{56,40},{64,... | collective-permute-start | bytes 835592 | tf_op jit(solution)/shard_map/ppermute | solution.py:162
  44.6 3.9 %collective-permute-done.4.refs_5_ = bf16[272,512]{1,0:T(8,128)(2,1)S(1)} collective-permute-done((bf16[272,512]{1,0:T(8,128)(2,1)S(1)}, bf16[272,512]{1,0:T(8,128)(2,1)S(1)}, u32[]{:S(2)}, u32[]{:S(2)}) %collective-permute-start.4) | collective-permute-done | bytes 278560 | tf_op jit(solution)/shard_map/ppermute | solution.py:161
  48.6 0.0 collective-permute-start.6
  48.6 0.0 collective-permute-done.5.refs_6_
  48.6 6.6 %collective-permute-done.6.refs_7_ = bf16[272,512]{1,0:T(8,128)(2,1)S(1)} collective-permute-done((bf16[272,512]{1,0:T(8,128)(2,1)S(1)}, bf16[272,512]{1,0:T(8,128)(2,1)S(1)}, u32[]{:S(2)}, u32[]{:S(2)}) %collective-permute-start.6) | collective-permute-done | bytes 278560 | tf_op jit(solution)/shard_map/ppermute | solution.py:164
  55.2 0.0 copy-start
  55.2 1.0 copy-done
  56.1 5.8 %place.1 = (bf16[1536,512]{1,0:T(8,128)(2,1)S(1)}, f32[1536,16]{1,0:T(8,128)S(1)}) custom-call(bf16[272,512]{1,0:T(8,128)(2,1)S(1)} %copy-done, bf16[272,512]{1,0:T(8,128)(2,1)S(1)} %collective-permute-done.refs_1_, bf16[272,512]{1,0:T(8,128)(2,1)S(1)} %collective-permute-done.1.refs_2_, bf16[272,512]{1,0:T(8,128)(2,1)S(1)} %collective-permute-done.2.refs_3_, ...), custom_call_target="tpu_custom_call" | custom-call | tf_op jit(solution)/shard_map/place/pallas_call | solution.py:167
  62.0 5.4 %collective-permute-start.7 = (bf16[1536,512]{1,0:T(8,128)(2,1)S(1)}, bf16[1536,512]{1,0:T(8,128)(2,1)S(1)}, u32[]{:S(2)}, u32[]{:S(2)}) collective-permute-start(bf16[1536,512]{1,0:T(8,128)(2,1)S(1)} %get-tuple-element.4.own_ref), channel_id=1, source_target_pairs={{0,8},{8,0},{16,24},{24,16},{32,40},{40,32},{48,56},{56,48},{64,72... | collective-permute-start | bytes 4718600 | tf_op jit(solution)/shard_map/ppermute | solution.py:175
  67.4 3.0 %collective-permute-done.7.other_ref = bf16[1536,512]{1,0:T(8,128)(2,1)S(1)} collective-permute-done((bf16[1536,512]{1,0:T(8,128)(2,1)S(1)}, bf16[1536,512]{1,0:T(8,128)(2,1)S(1)}, u32[]{:S(2)}, u32[]{:S(2)}) %collective-permute-start.7) | collective-permute-done | bytes 1572896 | tf_op jit(solution)/shard_map/ppermute | solution.py:175
  70.4 27.0 %score.1 = (f32[1536,32]{1,0:T(8,128)S(1)}, bf16[1536,4096]{1,0:T(8,128)(2,1)}) custom-call(bf16[1536,512]{1,0:T(8,128)(2,1)S(1)} %get-tuple-element.4.own_ref, bf16[1536,512]{1,0:T(8,128)(2,1)S(1)} %collective-permute-done.7.other_ref, f32[1536,16]{1,0:T(8,128)S(1)} %get-tuple-element.5.counts_ref, bf16[4096,1024]{1,0:T(8,128)(2,1)} %two_ref.1), custom_call_target="tpu_custom_call" | custom-call | tf_op jit(solution)/shard_map/score/pallas_call | solution.py:177
  97.5 0.9 copy.8
Async XLA Ops:
  23.5 11.3 %collective-permute-start = (bf16[272,512]{1,0:T(8,128)(2,1)}, bf16[272,512]{1,0:T(8,128)(2,1)S(1)}, u32[]{:S(2)}, u32[]{:S(2)}) collective-permute-start(bf16[272,512]{1,0:T(8,128)(2,1)} %block.1.refs_0_), channel_id=1, source_target_pairs={{0,16},{8,24},{16,32},{24,40},{32,48},{40,56},{48,64},{56,72},{64,... | collective-permute-start | bytes 835592 | tf_op jit(solution)/shard_map/ppermute | solution.py:161
  25.1 9.6 %collective-permute-start.1 = (bf16[272,512]{1,0:T(8,128)(2,1)}, bf16[272,512]{1,0:T(8,128)(2,1)S(1)}, u32[]{:S(2)}, u32[]{:S(2)}) collective-permute-start(bf16[272,512]{1,0:T(8,128)(2,1)} %block.1.refs_0_), channel_id=1, source_target_pairs={{0,112},{8,120},{16,0},{24,8},{32,16},{40,24},{48,32},{56,40},{64,... | collective-permute-start | bytes 835592 | tf_op jit(solution)/shard_map/ppermute | solution.py:162
  34.7 7.2 %collective-permute-start.2 = (bf16[272,512]{1,0:T(8,128)(2,1)S(1)}, bf16[272,512]{1,0:T(8,128)(2,1)S(1)}, u32[]{:S(2)}, u32[]{:S(2)}) collective-permute-start(bf16[272,512]{1,0:T(8,128)(2,1)S(1)} %collective-permute-done.refs_1_), channel_id=1, source_target_pairs={{0,16},{8,24},{16,32},{24,40},{32,48},{40,56},{48,64},{56,72},{64,... | collective-permute-start | bytes 835592 | tf_op jit(solution)/shard_map/ppermute | solution.py:161
  34.7 7.2 %collective-permute-start.3 = (bf16[272,512]{1,0:T(8,128)(2,1)S(1)}, bf16[272,512]{1,0:T(8,128)(2,1)S(1)}, u32[]{:S(2)}, u32[]{:S(2)}) collective-permute-start(bf16[272,512]{1,0:T(8,128)(2,1)S(1)} %collective-permute-done.1.refs_2_), channel_id=1, source_target_pairs={{0,112},{8,120},{16,0},{24,8},{32,16},{40,24},{48,32},{56,40},{64,... | collective-permute-start | bytes 835592 | tf_op jit(solution)/shard_map/ppermute | solution.py:162
  42.0 6.6 %collective-permute-start.4 = (bf16[272,512]{1,0:T(8,128)(2,1)S(1)}, bf16[272,512]{1,0:T(8,128)(2,1)S(1)}, u32[]{:S(2)}, u32[]{:S(2)}) collective-permute-start(bf16[272,512]{1,0:T(8,128)(2,1)S(1)} %collective-permute-done.2.refs_3_), channel_id=1, source_target_pairs={{0,16},{8,24},{16,32},{24,40},{32,48},{40,56},{48,64},{56,72},{64,... | collective-permute-start | bytes 835592 | tf_op jit(solution)/shard_map/ppermute | solution.py:161
  42.0 6.6 %collective-permute-start.5 = (bf16[272,512]{1,0:T(8,128)(2,1)S(1)}, bf16[272,512]{1,0:T(8,128)(2,1)S(1)}, u32[]{:S(2)}, u32[]{:S(2)}) collective-permute-start(bf16[272,512]{1,0:T(8,128)(2,1)S(1)} %collective-permute-done.3.refs_4_), channel_id=1, source_target_pairs={{0,112},{8,120},{16,0},{24,8},{32,16},{40,24},{48,32},{56,40},{64,... | collective-permute-start | bytes 835592 | tf_op jit(solution)/shard_map/ppermute | solution.py:162
  48.6 6.6 %collective-permute-start.6 = (bf16[272,512]{1,0:T(8,128)(2,1)S(1)}, bf16[272,512]{1,0:T(8,128)(2,1)S(1)}, u32[]{:S(2)}, u32[]{:S(2)}) collective-permute-start(bf16[272,512]{1,0:T(8,128)(2,1)S(1)} %collective-permute-done.4.refs_5_), channel_id=1, source_target_pairs={{0,16},{8,24},{16,32},{24,40},{32,48},{40,56},{48,64},{56,72},{64,... | collective-permute-start | bytes 835592 | tf_op jit(solution)/shard_map/ppermute | solution.py:164
  55.2 1.0 copy-start
  62.0 8.5 %collective-permute-start.7 = (bf16[1536,512]{1,0:T(8,128)(2,1)S(1)}, bf16[1536,512]{1,0:T(8,128)(2,1)S(1)}, u32[]{:S(2)}, u32[]{:S(2)}) collective-permute-start(bf16[1536,512]{1,0:T(8,128)(2,1)S(1)} %get-tuple-element.4.own_ref), channel_id=1, source_target_pairs={{0,8},{8,0},{16,24},{24,16},{32,40},{40,32},{48,56},{56,48},{64,72... | collective-permute-start | bytes 4718600 | tf_op jit(solution)/shard_map/ppermute | solution.py:175

commit v2 on v1

v2 whole, which is shorter than its diff:
```python
import jax
import jax.numpy as jnp
from jax import lax
from jax.experimental import pallas as pl
from jax.experimental.pallas import tpu as pltpu
from jax.sharding import PartitionSpec as P

K1S = 1536
K2S = 4096
D = 1024
HALF = 512
SEGS = 32
CAP = 8
NARROW = 8
SLOTS = 256
BLOCK = 272
LANES = 128
F32 = jnp.float32
BF16 = jnp.bfloat16

ALL = ("wide", "narrow")


def wide_of(x, z, c):
    return (x * 8 + z % 8) * 2 + c


WIDES = [(x, z, c) for x in range(2) for z in range(8) for c in range(2)]
PLANES = [
    [wide_of(x, z, c) * NARROW + n for x in range(2) for c in range(2) for n in range(NARROW)]
    for z in range(8)
]
CORE_SWAP = [(wide_of(x, z, c), wide_of(x, z, 1 - c)) for x, z, c in WIDES]
Z_FIRST = [(wide_of(x, z, c), wide_of(x, z + 1 - 2 * c, c)) for x, z, c in WIDES]
Z_SECOND = [(wide_of(x, z, c), wide_of(x, z - 1 + 2 * c, c)) for x, z, c in WIDES]


def iota2(shape, axis):
    return lax.broadcasted_iota(jnp.int32, shape, axis)


def pack_kernel(points_ref, lengths_ref, owner_ref, rows_ref, out_ref):
    r, q = iota2((SEGS, SEGS), 0), iota2((SEGS, SEGS), 1)
    eye = (r == q).astype(F32)
    length_row = lengths_ref[...].astype(F32)
    id_row = rows_ref[...].astype(F32)
    owner_row = owner_ref[...].astype(F32)
    length = jnp.sum(eye * length_row, axis=1, keepdims=True)
    ends = jnp.sum(jnp.where(q <= r, length_row, 0.0), axis=1, keepdims=True)
    ids = jnp.sum(eye * id_row, axis=1, keepdims=True)
    owner = jnp.sum(eye * owner_row, axis=1, keepdims=True)
    position = iota2((SEGS, 256), 1).astype(F32)
    member = ((position >= ends - length) & (position < ends)).astype(BF16)
    runs = jnp.dot(member, points_ref[...], preferred_element_type=F32).astype(BF16)

    rank_row = jnp.sum(jnp.where((owner == owner_row) & (r < q), 1.0, 0.0), axis=0, keepdims=True)
    slot_row = owner_row * CAP + rank_row
    place = (iota2((NARROW * CAP, SEGS), 0).astype(F32) == slot_row).astype(BF16)
    slots = jnp.dot(place, runs, preferred_element_type=F32).astype(BF16)
    high = jnp.floor(ids * (1.0 / 16.0))
    low = ids - 16.0 * high
    lane = iota2((SEGS, LANES), 1)
    tags = jnp.where(lane == 0, high, jnp.where(lane == 1, low, jnp.where(lane == 2, length, 0.0)))
    tags = jnp.dot(place, tags.astype(BF16), preferred_element_type=F32).astype(BF16)
    per = NARROW * CAP
    for x in range(2):
        for c in range(2):
            at = pl.ds((x * 2 + c) * per, per)
            out_ref[at, :HALF] = slots[:, c * HALF : (c + 1) * HALF]
            out_ref[at, HALF:] = tags


def block_kernel(received_ref, out_ref):
    out_ref[:SLOTS, :] = received_ref[:, :HALF]
    tags = received_ref[:, HALF:].astype(F32)
    turned = jnp.concatenate([tags[:LANES].T[:16], tags[LANES:].T[:16]], axis=1)
    out_ref[SLOTS:, :SLOTS] = turned.astype(BF16)
    out_ref[SLOTS:, SLOTS:] = jnp.zeros((16, HALF - SLOTS), BF16)


CHUNK = 256
NT = (((1,), (1,)), ((), ()))


def hot_rows(i, ref):
    tags = ref[SLOTS:, :SLOTS]
    ids = tags[0:1].astype(F32) * 16.0 + tags[1:2].astype(F32)
    row = (iota2((CHUNK, SLOTS), 0) + i * CHUNK).astype(F32)
    return (row == ids).astype(BF16), tags


def chunk(i):
    return pl.ds(pl.multiple_of(i * CHUNK, CHUNK), CHUNK)


def place(i, blocks, total, count):
    for ref in blocks:
        hot, tags = hot_rows(i, ref)
        total += jnp.dot(hot, ref[:SLOTS, :], preferred_element_type=F32)
        count += lax.dot_general(hot, tags, NT, preferred_element_type=F32)
    return total, count


def place_early_kernel(*refs):
    blocks, sums_ref, counts_ref, token_ref = refs[:-3], refs[-3], refs[-2], refs[-1]

    @pl.loop(0, K1S // CHUNK)
    def _(i):
        at = chunk(i)
        sums_ref[at, :], counts_ref[at, :] = place(
            i, blocks, jnp.zeros((CHUNK, HALF), F32), jnp.zeros((CHUNK, 16), F32)
        )

    token_ref[...] = jnp.zeros_like(token_ref)


def place_late_kernel(*refs):
    blocks, early_ref, tally_ref, sums_ref, counts_ref, rounded_ref = refs[:-5], *refs[-5:]

    @pl.loop(0, K1S // CHUNK)
    def _(i):
        at = chunk(i)
        total, count = place(i, blocks, early_ref[at, :], tally_ref[at, :])
        sums_ref[at, :] = total
        counts_ref[at, :] = count
        rounded_ref[at, :] = total.astype(BF16)


TILE = 512


def score_kernel(
    mine_ref, partner_ref, counts_ref, last_ref, last_partner_ref, two_ref,
    means_ref, scores_ref, sums, inverse,
):
    w = lax.axis_index("wide")
    core = w % 2

    @pl.when(pl.program_id(0) == 0)
    def _():
        @pl.loop(0, K1S // CHUNK)
        def _(i):
            at = chunk(i)
            hot, tags = hot_rows(i, last_ref)
            counts = counts_ref[at, :] + lax.dot_general(hot, tags, NT, preferred_element_type=F32)
            mine = mine_ref[at, :] + jnp.dot(hot, last_ref[:SLOTS, :], preferred_element_type=F32)
            other = partner_ref[at, :].astype(F32) + jnp.dot(
                hot, last_partner_ref[:SLOTS, :], preferred_element_type=F32
            )
            sums[at, pl.ds(pl.multiple_of(core * HALF, HALF), HALF)] = mine.astype(BF16)
            sums[at, pl.ds(pl.multiple_of((1 - core) * HALF, HALF), HALF)] = other.astype(BF16)
            square = jnp.sum(mine * mine + other * other, axis=1, keepdims=True)
            inverse[at, :] = jnp.broadcast_to(1.0 / jnp.sqrt(square + 1e-06), (CHUNK, LANES))
            lanes = pl.ds(pl.multiple_of(w // 4 * LANES, LANES), LANES)
            mean = pltpu.roll(sums[at, lanes].astype(F32), (4 - w % 4) % 4 * 32, 1)
            means_ref[:, at] = (mean / jnp.maximum(counts[:, 2:3], 1.0)).T[:32]

    product = lax.dot_general(sums[...], two_ref[...], NT, preferred_element_type=F32)
    scale = jnp.concatenate([inverse[...]] * (TILE // LANES), axis=1)
    scores_ref[...] = (product * scale).astype(BF16)


def whole(shape):
    return pl.BlockSpec(shape, lambda *_: (0,) * len(shape))


def cost(flops, moved):
    return pl.CostEstimate(flops=flops, bytes_accessed=moved, transcendentals=0)


def both(first, second):
    first = lax.ppermute(first, "wide", Z_FIRST)
    second = lax.ppermute(second, "wide", Z_SECOND)
    return lax.optimization_barrier((first, second))


def local(points, seg_lengths, seg_owner, seg_row, level_two):
    vmem = pl.BlockSpec(memory_space=pltpu.VMEM)
    send = pl.pallas_call(
        pack_kernel,
        out_shape=jax.ShapeDtypeStruct((SLOTS, HALF + LANES), BF16),
        in_specs=[vmem] * 4,
        out_specs=vmem,
        name="pack",
    )(points, seg_lengths, seg_owner.reshape(1, SEGS), seg_row)
    received = lax.all_to_all(send, ALL, 0, 0, axis_index_groups=PLANES, tiled=True)
    block = pl.pallas_call(
        block_kernel,
        out_shape=jax.ShapeDtypeStruct((BLOCK, HALF), BF16),
        in_specs=[vmem],
        out_specs=vmem,
        name="block",
    )(received)

    first = second = block
    blocks = [block]
    for _ in range(2):
        first, second = both(first, second)
        blocks += [first, second]

    totals = jax.ShapeDtypeStruct((K1S, HALF), F32)
    tallies = jax.ShapeDtypeStruct((K1S, 16), F32)
    small = pltpu.CompilerParams(vmem_limit_bytes=16 << 20)
    early, tally, token = pl.pallas_call(
        place_early_kernel,
        out_shape=(totals, tallies, jax.ShapeDtypeStruct((8, LANES), F32)),
        in_specs=[vmem] * 5,
        out_specs=(vmem, vmem, vmem),
        compiler_params=small,
        cost_estimate=cost(4 << 30, 4 << 20),
        name="place_early",
    )(*blocks)
    first, second = both(first, second)
    first, second, token = lax.optimization_barrier((first, second, token))
    last = lax.ppermute(first, "wide", Z_FIRST)
    mine, counts, rounded = pl.pallas_call(
        place_late_kernel,
        out_shape=(totals, tallies, jax.ShapeDtypeStruct((K1S, HALF), BF16)),
        in_specs=[vmem] * 4,
        out_specs=(vmem, vmem, vmem),
        compiler_params=small,
        cost_estimate=cost(4 << 30, 4 << 20),
        name="place_late",
    )(first, second, early, tally)
    partner = lax.ppermute(rounded, "wide", CORE_SWAP)
    last, partner = lax.optimization_barrier((last, partner))
    last_partner = lax.ppermute(last, "wide", CORE_SWAP)

    means, scores = pl.pallas_call(
        score_kernel,
        grid=(K2S // TILE,),
        out_shape=(
            jax.ShapeDtypeStruct((32, K1S), F32),
            jax.ShapeDtypeStruct((K1S, K2S), BF16),
        ),
        in_specs=[
            whole((K1S, HALF)),
            whole((K1S, HALF)),
            whole((K1S, 16)),
            whole((BLOCK, HALF)),
            whole((BLOCK, HALF)),
            pl.BlockSpec((TILE, D), lambda j: (j, 0)),
        ],
        out_specs=(whole((32, K1S)), pl.BlockSpec((K1S, TILE), lambda j: (0, j))),
        scratch_shapes=[pltpu.VMEM((K1S, D), BF16), pltpu.VMEM((K1S, LANES), F32)],
        compiler_params=pltpu.CompilerParams(vmem_limit_bytes=40 << 20),
        cost_estimate=cost(14 << 30, 24 << 20),
        name="score",
    )(mine, partner, counts, last, last_partner, level_two)
    return means.T, scores


def solution(mesh):
    return jax.shard_map(
        local,
        mesh=mesh,
        in_specs=(
            P(ALL, None),
            P(ALL, None),
            P(ALL, None, None),
            P(ALL, None),
            P("wide", None),
        ),
        out_specs=(P("narrow", "wide"), P("narrow", "wide")),
        check_vma=False,
    )
```

time: 99.6 us -> 86.5 us (0.87)
  Pallas kernels: 36.8 us -> 29.7 us
  waiting for transfers between devices: 23.8 us -> 17.7 us
  local copies, waits for them, and re-layouts: 3.22 us -> 0.96 us
  starting transfers between devices: 16.4 us -> 18.6 us
    pallas_call x1, Pallas kernels: 27 us -> 19.1 us  [local(): pl.pallas_call(score_kernel, grid=(K2S // TILE,), out_shape=(jax.ShapeDty...]
    ppermute x8 -> x9, waiting for transfers between devices: 23.8 us -> 17.7 us  [the longest x3 8.37 us: both(): second = lax.ppermute(second, 'wide', Z_SECOND)]
    ppermute x8 -> x9, starting transfers between devices: 16.4 us -> 18.6 us  [the longest x3 7.05 us: both(): first = lax.ppermute(first, 'wide', Z_FIRST)]
    unnamed x3 -> x6, local copies, waits for them, and re-layouts: 2.3 us -> 0.96 us
    pallas_call x1 -> x2, Pallas kernels: 5.8 us -> 6.65 us  [the longest x1 4.52 us: local(): pl.pallas_call(place_early_kernel, out_shape=(totals, tallies, jax.ShapeD...]
  transfers between devices with their start and end apart: 8 -> 9, of which waited for: 5 -> 6; matrix products, arithmetic and copies ran while one was open for 0% -> 0% of each run, Pallas kernels for 0% -> 5%
where the time goes in v2:
time: 86.5 us; the launch traced here: 85.2 us
  Pallas kernels  29.7 us (34%)
  starting transfers between devices  18.6 us (22%)
  waiting for transfers between devices  17.7 us (20%)
  blocking collectives  17.5 us (20%)
  local copies, waits for them, and re-layouts  0.96 us (1%)
    pallas_call x1, Pallas kernels, local(): pl.pallas_call(score_kernel, grid=(K2S // TILE,), out_shape=(jax.ShapeDty...  19.1 us
    all_to_all x1, blocking collectives, local(): lax.all_to_all(send, ALL, 0, 0, axis_index_groups=PLANES, tiled=True)  17.5 us
    ppermute x3, waiting for transfers between devices, both(): second = lax.ppermute(second, 'wide', Z_SECOND)  8.37 us
    ppermute x3, starting transfers between devices, both(): first = lax.ppermute(first, 'wide', Z_FIRST)  7.05 us
    pallas_call x1, Pallas kernels, local(): pl.pallas_call(place_early_kernel, out_shape=(totals, tallies, jax.ShapeD...  4.52 us
    ppermute x1, starting transfers between devices, local(): partner = lax.ppermute(rounded, 'wide', CORE_SWAP)  4.42 us
    ppermute x3, waiting for transfers between devices, both(): first = lax.ppermute(first, 'wide', Z_FIRST)  4.4 us
    ppermute x1, waiting for transfers between devices, local(): last = lax.ppermute(first, 'wide', Z_FIRST)  3.71 us
  transfers between devices with their start and end apart: 9, of which 6 were waited for; matrix products, arithmetic and copies ran while one was open for 0% of the time, Pallas kernels for 5%

profile of v2, /device:TPU:1, one launch (start us, length us, event | category | flops | bytes accessed | tf_op | source)
XLA Modules:
  0.0 85.2 jit_solution(16189665788451391345)
XLA Ops:
  0.6 2.2 %pack.1 = bf16[256,640]{1,0:T(8,128)(2,1)} custom-call(bf16[256,1024]{1,0:T(8,128)(2,1)} %points_ref.1, s32[1,32]{1,0:T(1,128)} %lengths_ref.1, s32[1,32]{1,0:T(1,128)} %bitcast.8, s32[1,32]{1,0:T(1,128)} %rows_ref.1), custom_call_target="tpu_custom_call" | custom-call | tf_op jit(solution)/shard_map/pack/pallas_call | solution.py:179
  2.8 17.5 %all_to_all.11 = bf16[32,8,640]{2,1,0:T(8,128)(2,1)} all-to-all(bf16[32,8,640]{2,1,0:T(8,128)(2,1)} %bitcast.7), channel_id=1, replica_groups={{0,1,2,3,4,5,6,7,8,9,10,11,12,13,14,15,128,129,130,131,132,133,134,135,..., dimensions={0} | all-to-all | bytes 655360 | tf_op jit(solution)/shard_map/all_to_all | solution.py:186
  20.3 1.8 %block.1.refs_0_ = bf16[272,512]{1,0:T(8,128)(2,1)} custom-call(bf16[256,640]{1,0:T(8,128)(2,1)} %bitcast.6), custom_call_target="tpu_custom_call" | custom-call | tf_op jit(solution)/shard_map/block/pallas_call | solution.py:187
  22.1 1.6 %collective-permute-start.1 = (bf16[272,512]{1,0:T(8,128)(2,1)}, bf16[272,512]{1,0:T(8,128)(2,1)S(1)}, u32[]{:S(2)}, u32[]{:S(2)}) collective-permute-start(bf16[272,512]{1,0:T(8,128)(2,1)} %block.1.refs_0_), channel_id=1, source_target_pairs={{0,112},{8,24},{16,0},{24,40},{32,16},{40,56},{48,32},{56,72},{64,... | collective-permute-start | bytes 835592 | tf_op jit(solution)/shard_map/ppermute | solution.py:173
  23.7 3.9 %collective-permute-start = (bf16[272,512]{1,0:T(8,128)(2,1)}, bf16[272,512]{1,0:T(8,128)(2,1)S(1)}, u32[]{:S(2)}, u32[]{:S(2)}) collective-permute-start(bf16[272,512]{1,0:T(8,128)(2,1)} %block.1.refs_0_), channel_id=1, source_target_pairs={{0,16},{8,120},{16,32},{24,8},{32,48},{40,24},{48,64},{56,40},{64,... | collective-permute-start | bytes 835592 | tf_op jit(solution)/shard_map/ppermute | solution.py:172
  27.7 4.1 %collective-permute-done.1.refs_2_ = bf16[272,512]{1,0:T(8,128)(2,1)S(1)} collective-permute-done((bf16[272,512]{1,0:T(8,128)(2,1)}, bf16[272,512]{1,0:T(8,128)(2,1)S(1)}, u32[]{:S(2)}, u32[]{:S(2)}) %collective-permute-start.1) | collective-permute-done | bytes 278560 | tf_op jit(solution)/shard_map/ppermute | solution.py:173
  31.8 0.9 %collective-permute-done.refs_1_ = bf16[272,512]{1,0:T(8,128)(2,1)S(1)} collective-permute-done((bf16[272,512]{1,0:T(8,128)(2,1)}, bf16[272,512]{1,0:T(8,128)(2,1)S(1)}, u32[]{:S(2)}, u32[]{:S(2)}) %collective-permute-start) | collective-permute-done | bytes 278560 | tf_op jit(solution)/shard_map/ppermute | solution.py:172
  32.7 3.0 %collective-permute-start.2 = (bf16[272,512]{1,0:T(8,128)(2,1)S(1)}, bf16[272,512]{1,0:T(8,128)(2,1)S(1)}, u32[]{:S(2)}, u32[]{:S(2)}) collective-permute-start(bf16[272,512]{1,0:T(8,128)(2,1)S(1)} %collective-permute-done.refs_1_), channel_id=1, source_target_pairs={{0,16},{8,120},{16,32},{24,8},{32,48},{40,24},{48,64},{56,40},{64,... | collective-permute-start | bytes 835592 | tf_op jit(solution)/shard_map/ppermute | solution.py:172
  35.8 0.0 collective-permute-start.3
  35.8 3.5 %collective-permute-done.2.refs_3_ = bf16[272,512]{1,0:T(8,128)(2,1)S(1)} collective-permute-done((bf16[272,512]{1,0:T(8,128)(2,1)S(1)}, bf16[272,512]{1,0:T(8,128)(2,1)S(1)}, u32[]{:S(2)}, u32[]{:S(2)}) %collective-permute-start.2) | collective-permute-done | bytes 278560 | tf_op jit(solution)/shard_map/ppermute | solution.py:172
  39.3 4.2 %collective-permute-done.3.refs_4_ = bf16[272,512]{1,0:T(8,128)(2,1)S(1)} collective-permute-done((bf16[272,512]{1,0:T(8,128)(2,1)S(1)}, bf16[272,512]{1,0:T(8,128)(2,1)S(1)}, u32[]{:S(2)}, u32[]{:S(2)}) %collective-permute-start.3) | collective-permute-done | bytes 278560 | tf_op jit(solution)/shard_map/ppermute | solution.py:173
  43.5 0.1 collective-permute-start.4
  43.6 1.4 %collective-permute-start.5 = (bf16[272,512]{1,0:T(8,128)(2,1)S(1)}, bf16[272,512]{1,0:T(8,128)(2,1)S(1)}, u32[]{:S(2)}, u32[]{:S(2)}) collective-permute-start(bf16[272,512]{1,0:T(8,128)(2,1)S(1)} %collective-permute-done.3.refs_4_), channel_id=1, source_target_pairs={{0,112},{8,24},{16,0},{24,40},{32,16},{40,56},{48,32},{56,72},{64,... | collective-permute-start | bytes 835592 | tf_op jit(solution)/shard_map/ppermute | solution.py:173
  45.0 0.0 copy-start
  45.0 1.0 %copy-done = bf16[272,512]{1,0:T(8,128)(2,1)S(1)} copy-done((bf16[272,512]{1,0:T(8,128)(2,1)S(1)}, bf16[272,512]{1,0:T(8,128)(2,1)}, u32[]{:S(2)}) %copy-start) | copy-done | bytes 278552
  45.9 0.0 slice-start
  45.9 4.5 %place_early.1 = (f32[1536,512]{1,0:T(8,128)S(1)}, f32[1536,16]{1,0:T(8,128)S(1)}, f32[8,128]{1,0:T(8,128)}) custom-call(bf16[272,512]{1,0:T(8,128)(2,1)S(1)} %copy-done, bf16[272,512]{1,0:T(8,128)(2,1)S(1)} %collective-permute-done.refs_1_, bf16[272,512]{1,0:T(8,128)(2,1)S(1)} %collective-permute-done.1.refs_2_, ...), custom_call_target="tpu_custom_call" | custom-call | flops 4294967296 | bytes 4194304 | tf_op jit(solution)/shard_map/place_early/pallas_call | solution.py:204
  50.4 0.0 collective-permute-done.4.refs_0_
  50.4 0.0 collective-permute-done.5.refs_1_
  50.5 0.0 slice-start.1
  50.5 2.1 %place_late.1 = (f32[1536,512]{1,0:T(8,128)S(1)}, f32[1536,16]{1,0:T(8,128)S(1)}, bf16[1536,512]{1,0:T(8,128)(2,1)S(1)}) custom-call(bf16[272,512]{1,0:T(8,128)(2,1)S(1)} %collective-permute-done.4.refs_0_, bf16[272,512]{1,0:T(8,128)(2,1)S(1)} %collective-permute-done.5.refs_1_, f32[1536,512]{1,0:T(8,128)S(1)} %get-tuple-element.23.refs_2_, ...), custom_call_target="tpu_custom_call" | custom-call | flops 4294967296 | bytes 4194304 | tf_op jit(solution)/shard_map/place_late/pallas_call | solution.py:216
  52.6 4.4 %collective-permute-start.7 = (bf16[1536,512]{1,0:T(8,128)(2,1)S(1)}, bf16[1536,512]{1,0:T(8,128)(2,1)S(1)}, u32[]{:S(2)}, u32[]{:S(2)}) collective-permute-start(bf16[1536,512]{1,0:T(8,128)(2,1)S(1)} %get-tuple-element.26), channel_id=1, source_target_pairs={{0,8},{8,0},{16,24},{24,16},{32,40},{40,32},{48,56},{56,48},{64,72... | collective-permute-start | bytes 4718600 | tf_op jit(solution)/shard_map/ppermute | solution.py:225
  57.0 2.0 %collective-permute-start.6 = (bf16[272,512]{1,0:T(8,128)(2,1)S(1)}, bf16[272,512]{1,0:T(8,128)(2,1)S(1)}, u32[]{:S(2)}, u32[]{:S(2)}) collective-permute-start(bf16[272,512]{1,0:T(8,128)(2,1)S(1)} %collective-permute-done.4.refs_0_), channel_id=1, source_target_pairs={{0,16},{8,120},{16,32},{24,8},{32,48},{40,24},{48,64},{56,40},{64,... | collective-permute-start | bytes 835592 | tf_op jit(solution)/shard_map/ppermute | solution.py:215
  59.0 3.7 %collective-permute-done.6.last_ref = bf16[272,512]{1,0:T(8,128)(2,1)S(1)} collective-permute-done((bf16[272,512]{1,0:T(8,128)(2,1)S(1)}, bf16[272,512]{1,0:T(8,128)(2,1)S(1)}, u32[]{:S(2)}, u32[]{:S(2)}) %collective-permute-start.6) | collective-permute-done | bytes 278560 | tf_op jit(solution)/shard_map/ppermute | solution.py:215
  62.7 0.0 collective-permute-done.7.partner_ref
  62.7 2.2 %collective-permute-start.8 = (bf16[272,512]{1,0:T(8,128)(2,1)S(1)}, bf16[272,512]{1,0:T(8,128)(2,1)S(1)}, u32[]{:S(2)}, u32[]{:S(2)}) collective-permute-start(bf16[272,512]{1,0:T(8,128)(2,1)S(1)} %collective-permute-done.6.last_ref), channel_id=1, source_target_pairs={{0,8},{8,0},{16,24},{24,16},{32,40},{40,32},{48,56},{56,48},{64,72... | collective-permute-start | bytes 835592 | tf_op jit(solution)/shard_map/ppermute | solution.py:227
  64.9 1.2 %collective-permute-done.8.last_partner_ref = bf16[272,512]{1,0:T(8,128)(2,1)S(1)} collective-permute-done((bf16[272,512]{1,0:T(8,128)(2,1)S(1)}, bf16[272,512]{1,0:T(8,128)(2,1)S(1)}, u32[]{:S(2)}, u32[]{:S(2)}) %collective-permute-start.8) | collective-permute-done | bytes 278560 | tf_op jit(solution)/shard_map/ppermute | solution.py:227
  66.1 0.0 slice-done
  66.1 0.0 slice-done.1
  66.1 19.1 %score.1 = (f32[32,1536]{1,0:T(8,128)}, bf16[1536,4096]{1,0:T(8,128)(2,1)}) custom-call(f32[1536,512]{1,0:T(8,128)S(1)} %get-tuple-element.25.mine_ref, bf16[1536,512]{1,0:T(8,128)(2,1)S(1)} %collective-permute-done.7.partner_ref, f32[1536,16]{1,0:T(8,128)S(1)} %get-tuple-element.28.counts_ref, bf16[272,512]{1,0:T(8,128)(2,1)S(1)} %collective-permute-done.6.last_ref, ...), custom_call_target="tpu_custom_call" | custom-call | flops 15032385536 | bytes 25165824 | tf_op jit(solution)/shard_map/score/pallas_call | solution.py:229
  (1 shorter events, 0.0 us)
Async XLA Ops:
  22.1 9.7 %collective-permute-start.1 = (bf16[272,512]{1,0:T(8,128)(2,1)}, bf16[272,512]{1,0:T(8,128)(2,1)S(1)}, u32[]{:S(2)}, u32[]{:S(2)}) collective-permute-start(bf16[272,512]{1,0:T(8,128)(2,1)} %block.1.refs_0_), channel_id=1, source_target_pairs={{0,112},{8,24},{16,0},{24,40},{32,16},{40,56},{48,32},{56,72},{64,... | collective-permute-start | bytes 835592 | tf_op jit(solution)/shard_map/ppermute | solution.py:173
  23.7 9.0 %collective-permute-start = (bf16[272,512]{1,0:T(8,128)(2,1)}, bf16[272,512]{1,0:T(8,128)(2,1)S(1)}, u32[]{:S(2)}, u32[]{:S(2)}) collective-permute-start(bf16[272,512]{1,0:T(8,128)(2,1)} %block.1.refs_0_), channel_id=1, source_target_pairs={{0,16},{8,120},{16,32},{24,8},{32,48},{40,24},{48,64},{56,40},{64,... | collective-permute-start | bytes 835592 | tf_op jit(solution)/shard_map/ppermute | solution.py:172
  32.7 6.5 %collective-permute-start.2 = (bf16[272,512]{1,0:T(8,128)(2,1)S(1)}, bf16[272,512]{1,0:T(8,128)(2,1)S(1)}, u32[]{:S(2)}, u32[]{:S(2)}) collective-permute-start(bf16[272,512]{1,0:T(8,128)(2,1)S(1)} %collective-permute-done.refs_1_), channel_id=1, source_target_pairs={{0,16},{8,120},{16,32},{24,8},{32,48},{40,24},{48,64},{56,40},{64,... | collective-permute-start | bytes 835592 | tf_op jit(solution)/shard_map/ppermute | solution.py:172
  35.8 7.7 %collective-permute-start.3 = (bf16[272,512]{1,0:T(8,128)(2,1)S(1)}, bf16[272,512]{1,0:T(8,128)(2,1)S(1)}, u32[]{:S(2)}, u32[]{:S(2)}) collective-permute-start(bf16[272,512]{1,0:T(8,128)(2,1)S(1)} %collective-permute-done.1.refs_2_), channel_id=1, source_target_pairs={{0,112},{8,24},{16,0},{24,40},{32,16},{40,56},{48,32},{56,72},{64,... | collective-permute-start | bytes 835592 | tf_op jit(solution)/shard_map/ppermute | solution.py:173
  43.5 7.0 %collective-permute-start.4 = (bf16[272,512]{1,0:T(8,128)(2,1)S(1)}, bf16[272,512]{1,0:T(8,128)(2,1)S(1)}, u32[]{:S(2)}, u32[]{:S(2)}) collective-permute-start(bf16[272,512]{1,0:T(8,128)(2,1)S(1)} %collective-permute-done.2.refs_3_), channel_id=1, source_target_pairs={{0,16},{8,120},{16,32},{24,8},{32,48},{40,24},{48,64},{56,40},{64,... | collective-permute-start | bytes 835592 | tf_op jit(solution)/shard_map/ppermute | solution.py:172
  43.6 6.9 %collective-permute-start.5 = (bf16[272,512]{1,0:T(8,128)(2,1)S(1)}, bf16[272,512]{1,0:T(8,128)(2,1)S(1)}, u32[]{:S(2)}, u32[]{:S(2)}) collective-permute-start(bf16[272,512]{1,0:T(8,128)(2,1)S(1)} %collective-permute-done.3.refs_4_), channel_id=1, source_target_pairs={{0,112},{8,24},{16,0},{24,40},{32,16},{40,56},{48,32},{56,72},{64,... | collective-permute-start | bytes 835592 | tf_op jit(solution)/shard_map/ppermute | solution.py:173
  45.0 1.0 %copy-start = (bf16[272,512]{1,0:T(8,128)(2,1)S(1)}, bf16[272,512]{1,0:T(8,128)(2,1)}, u32[]{:S(2)}) copy-start(bf16[272,512]{1,0:T(8,128)(2,1)} %block.1.refs_0_) | copy-start | bytes 835588
  45.9 20.1 %slice-start = ((s8[8388608]{0:T(1024)(128)(4,1)}), s8[4194304]{0:T(1024)(128)(4,1)S(1)}, s32[]{:S(2)}) async-start(s8[8388608]{0:T(1024)(128)(4,1)} %bitcast.4), calls=%async_computation.1 | async-start | bytes 8388608
  50.5 15.6 %slice-start.1 = ((s8[8388608]{0:T(1024)(128)(4,1)}), s8[4194304]{0:T(1024)(128)(4,1)S(1)}, s32[]{:S(2)}) async-start(s8[8388608]{0:T(1024)(128)(4,1)} %bitcast.4), calls=%async_computation.2 | async-start | bytes 8388608
  52.6 10.1 %collective-permute-start.7 = (bf16[1536,512]{1,0:T(8,128)(2,1)S(1)}, bf16[1536,512]{1,0:T(8,128)(2,1)S(1)}, u32[]{:S(2)}, u32[]{:S(2)}) collective-permute-start(bf16[1536,512]{1,0:T(8,128)(2,1)S(1)} %get-tuple-element.26), channel_id=1, source_target_pairs={{0,8},{8,0},{16,24},{24,16},{32,40},{40,32},{48,56},{56,48},{64,72... | collective-permute-start | bytes 4718600 | tf_op jit(solution)/shard_map/ppermute | solution.py:225
  57.0 5.7 %collective-permute-start.6 = (bf16[272,512]{1,0:T(8,128)(2,1)S(1)}, bf16[272,512]{1,0:T(8,128)(2,1)S(1)}, u32[]{:S(2)}, u32[]{:S(2)}) collective-permute-start(bf16[272,512]{1,0:T(8,128)(2,1)S(1)} %collective-permute-done.4.refs_0_), channel_id=1, source_target_pairs={{0,16},{8,120},{16,32},{24,8},{32,48},{40,24},{48,64},{56,40},{64,... | collective-permute-start | bytes 835592 | tf_op jit(solution)/shard_map/ppermute | solution.py:215
  62.7 3.3 %collective-permute-start.8 = (bf16[272,512]{1,0:T(8,128)(2,1)S(1)}, bf16[272,512]{1,0:T(8,128)(2,1)S(1)}, u32[]{:S(2)}, u32[]{:S(2)}) collective-permute-start(bf16[272,512]{1,0:T(8,128)(2,1)S(1)} %collective-permute-done.6.last_ref), channel_id=1, source_target_pairs={{0,8},{8,0},{16,24},{24,16},{32,40},{40,32},{48,56},{56,48},{64,72... | collective-permute-start | bytes 835592 | tf_op jit(solution)/shard_map/ppermute | solution.py:227

commit v3 on v2

v3 whole, which is shorter than its diff:
```python
import jax
import jax.numpy as jnp
from jax import lax
from jax.experimental import pallas as pl
from jax.experimental.pallas import tpu as pltpu
from jax.sharding import PartitionSpec as P

K1S = 1536
K2S = 4096
D = 1024
HALF = 512
SEGS = 32
CAP = 8
NARROW = 8
SLOTS = 256
BLOCK = 272
LANES = 128
F32 = jnp.float32
BF16 = jnp.bfloat16

ALL = ("wide", "narrow")


def wide_of(x, z, c):
    return (x * 8 + z % 8) * 2 + c


WIDES = [(x, z, c) for x in range(2) for z in range(8) for c in range(2)]
PLANES = [
    [wide_of(x, z, c) * NARROW + n for x in range(2) for c in range(2) for n in range(NARROW)]
    for z in range(8)
]
CORE_SWAP = [(wide_of(x, z, c), wide_of(x, z, 1 - c)) for x, z, c in WIDES]
Z_UP = [(wide_of(x, z, c), wide_of(x, z + 1, c)) for x, z, c in WIDES]
Z_DOWN = [(wide_of(x, z, c), wide_of(x, z - 1, c)) for x, z, c in WIDES]


def iota2(shape, axis):
    return lax.broadcasted_iota(jnp.int32, shape, axis)


def pack_kernel(points_ref, lengths_ref, owner_ref, rows_ref, out_ref):
    r, q = iota2((SEGS, SEGS), 0), iota2((SEGS, SEGS), 1)
    eye = (r == q).astype(F32)
    length_row = lengths_ref[...].astype(F32)
    id_row = rows_ref[...].astype(F32)
    owner_row = owner_ref[...].astype(F32)
    length = jnp.sum(eye * length_row, axis=1, keepdims=True)
    ends = jnp.sum(jnp.where(q <= r, length_row, 0.0), axis=1, keepdims=True)
    ids = jnp.sum(eye * id_row, axis=1, keepdims=True)
    owner = jnp.sum(eye * owner_row, axis=1, keepdims=True)
    position = iota2((SEGS, 256), 1).astype(F32)
    member = ((position >= ends - length) & (position < ends)).astype(BF16)
    runs = jnp.dot(member, points_ref[...], preferred_element_type=F32).astype(BF16)

    rank_row = jnp.sum(jnp.where((owner == owner_row) & (r < q), 1.0, 0.0), axis=0, keepdims=True)
    slot_row = owner_row * CAP + rank_row
    place = (iota2((NARROW * CAP, SEGS), 0).astype(F32) == slot_row).astype(BF16)
    slots = jnp.dot(place, runs, preferred_element_type=F32).astype(BF16)
    high = jnp.floor(ids * (1.0 / 16.0))
    low = ids - 16.0 * high
    lane = iota2((SEGS, LANES), 1)
    tags = jnp.where(lane == 0, high, jnp.where(lane == 1, low, jnp.where(lane == 2, length, 0.0)))
    tags = jnp.dot(place, tags.astype(BF16), preferred_element_type=F32).astype(BF16)
    per = NARROW * CAP
    for x in range(2):
        for c in range(2):
            at = pl.ds((x * 2 + c) * per, per)
            out_ref[at, :HALF] = slots[:, c * HALF : (c + 1) * HALF]
            out_ref[at, HALF:] = tags


def block_kernel(received_ref, out_ref):
    out_ref[:SLOTS, :] = received_ref[:, :HALF]
    tags = received_ref[:, HALF:].astype(F32)
    turned = jnp.concatenate([tags[:LANES].T[:16], tags[LANES:].T[:16]], axis=1)
    out_ref[SLOTS:, :SLOTS] = turned.astype(BF16)
    out_ref[SLOTS:, SLOTS:] = jnp.zeros((16, HALF - SLOTS), BF16)


CHUNK = 256
NT = (((1,), (1,)), ((), ()))


def hot_rows(start, rows, ref):
    tags = ref[SLOTS:, :SLOTS]
    ids = tags[0:1].astype(F32) * 16.0 + tags[1:2].astype(F32)
    row = (iota2((rows, SLOTS), 0) + start).astype(F32)
    return (row == ids).astype(BF16), tags


def chunk(i):
    return pl.ds(pl.multiple_of(i * CHUNK, CHUNK), CHUNK)


def place(i, blocks, total):
    for ref in blocks:
        total += jnp.dot(hot_rows(i * CHUNK, CHUNK, ref)[0], ref[:SLOTS, :], preferred_element_type=F32)
    return total


def place_early_kernel(*refs):
    blocks, sums_ref = refs[:-1], refs[-1]

    @pl.loop(0, K1S // CHUNK)
    def _(i):
        sums_ref[chunk(i), :] = place(i, blocks, jnp.zeros((CHUNK, HALF), F32))


def place_late_kernel(*refs):
    blocks, early_ref, sums_ref, rounded_ref = refs[:-3], *refs[-3:]

    @pl.loop(0, K1S // CHUNK)
    def _(i):
        total = place(i, blocks, early_ref[chunk(i), :])
        sums_ref[chunk(i), :] = total
        rounded_ref[chunk(i), :] = total.astype(BF16)


def count_kernel(*refs):
    blocks, counts_ref = refs[:-1], refs[-1]

    @pl.loop(0, K1S // CHUNK)
    def _(i):
        count = jnp.zeros((CHUNK, 16), F32)
        for ref in blocks:
            hot, tags = hot_rows(i * CHUNK, CHUNK, ref)
            count += lax.dot_general(hot, tags, NT, preferred_element_type=F32)
        counts_ref[chunk(i), :] = count


TILE = 512
PART = 768


def finish_kernel(sums_ref, tally_ref, last_ref, mine_ref, squares_ref, counts_ref):
    @pl.loop(0, K1S // CHUNK)
    def _(i):
        at = chunk(i)
        hot, tags = hot_rows(i * CHUNK, CHUNK, last_ref)
        counts_ref[at, :] = tally_ref[at, :] + lax.dot_general(hot, tags, NT, preferred_element_type=F32)
        mine = sums_ref[at, :] + jnp.dot(hot, last_ref[:SLOTS, :], preferred_element_type=F32)
        square = jnp.sum(mine * mine, axis=1, keepdims=True)
        mine_ref[at, :] = mine.astype(BF16)
        squares_ref[at, :] = jnp.broadcast_to(square, (CHUNK, LANES))


def score_kernel(
    mine_ref, squares_ref, counts_ref, partner_ref, last_ref, last_partner_ref, two_ref,
    means_ref, scores_ref, sums, inverse,
):
    w = lax.axis_index("wide")
    core = w % 2

    def score(at):
        product = lax.dot_general(sums[at, :], two_ref[...], NT, preferred_element_type=F32)
        scale = jnp.concatenate([inverse[at, :]] * (TILE // LANES), axis=1)
        scores_ref[at, :] = (product * scale).astype(BF16)

    @pl.when(pl.program_id(0) == 0)
    def _():
        for start in range(0, K1S, PART):
            at = pl.ds(start, PART)
            hot, _ = hot_rows(start, PART, last_ref)
            partner = partner_ref[at, :].astype(F32) + jnp.dot(
                hot, last_partner_ref[:SLOTS, :], preferred_element_type=F32
            )
            sums[at, pl.ds(pl.multiple_of(core * HALF, HALF), HALF)] = mine_ref[at, :]
            sums[at, pl.ds(pl.multiple_of((1 - core) * HALF, HALF), HALF)] = partner.astype(BF16)
            square = squares_ref[at, :] + jnp.sum(partner * partner, axis=1, keepdims=True)
            inverse[at, :] = 1.0 / jnp.sqrt(square + 1e-06)
            lanes = pl.ds(pl.multiple_of(w // 4 * LANES, LANES), LANES)
            mean = pltpu.roll(sums[at, lanes].astype(F32), (4 - w % 4) % 4 * 32, 1)
            means_ref[:, at] = (mean / jnp.maximum(counts_ref[at, 2:3], 1.0)).T[:32]
            score(at)

    @pl.when(pl.program_id(0) > 0)
    def _():
        score(pl.ds(0, K1S))


def whole(shape):
    return pl.BlockSpec(shape, lambda *_: (0,) * len(shape), pipeline_mode=pl.Buffered(1))


def cost(flops, moved):
    return pl.CostEstimate(flops=flops, bytes_accessed=moved, transcendentals=0)


def local(points, seg_lengths, seg_owner, seg_row, level_two):
    vmem = pl.BlockSpec(memory_space=pltpu.VMEM)
    send = pl.pallas_call(
        pack_kernel,
        out_shape=jax.ShapeDtypeStruct((SLOTS, HALF + LANES), BF16),
        in_specs=[vmem] * 4,
        out_specs=vmem,
        name="pack",
    )(points, seg_lengths, seg_owner.reshape(1, SEGS), seg_row)
    received = lax.all_to_all(send, ALL, 0, 0, axis_index_groups=PLANES, tiled=True)
    block = pl.pallas_call(
        block_kernel,
        out_shape=jax.ShapeDtypeStruct((BLOCK, HALF), BF16),
        in_specs=[vmem],
        out_specs=vmem,
        name="block",
    )(received)

    def placer(kernel, flops, out_shape, *operands):
        return pl.pallas_call(
            kernel,
            out_shape=out_shape,
            in_specs=[vmem] * len(operands),
            out_specs=jax.tree.map(lambda _: vmem, out_shape),
            compiler_params=pltpu.CompilerParams(vmem_limit_bytes=16 << 20),
            cost_estimate=cost(flops, 4 << 20),
            name=kernel.__name__[:-7],
        )(*operands)

    up = down = block
    blocks = [block]
    for _ in range(3):
        up, down = lax.ppermute(up, "wide", Z_UP), lax.ppermute(down, "wide", Z_DOWN)
        blocks += [up, down]
    last = lax.ppermute(down, "wide", Z_DOWN)

    totals, halves, tallies, squares_shape = [
        jax.ShapeDtypeStruct((K1S, n), t) for n, t in ((HALF, F32), (HALF, BF16), (16, F32), (LANES, F32))
    ]
    early = placer(place_early_kernel, 3 << 30, totals, *blocks[:5])
    sums, rounded = placer(place_late_kernel, 24 << 30, (totals, halves), up, down, early)
    partner = lax.ppermute(rounded, "wide", CORE_SWAP)
    tally = placer(count_kernel, 1 << 20, tallies, *blocks)
    last_partner = lax.ppermute(last, "wide", CORE_SWAP)
    mine, squares, counts = placer(
        finish_kernel, 24 << 30, (halves, squares_shape, tallies), sums, tally, last
    )

    means, scores = pl.pallas_call(
        score_kernel,
        grid=(K2S // TILE,),
        out_shape=(
            jax.ShapeDtypeStruct((32, K1S), F32),
            jax.ShapeDtypeStruct((K1S, K2S), BF16),
        ),
        in_specs=[
            *[vmem] * 6,
            pl.BlockSpec((TILE, D), lambda j: (j, 0)),
        ],
        out_specs=(whole((32, K1S)), pl.BlockSpec((K1S, TILE), lambda j: (0, j))),
        scratch_shapes=[pltpu.VMEM((K1S, D), BF16), pltpu.VMEM((K1S, LANES), F32)],
        compiler_params=pltpu.CompilerParams(vmem_limit_bytes=24 << 20),
        cost_estimate=cost(14 << 30, 24 << 20),
        name="score",
    )(mine, squares, counts, partner, last, last_partner, level_two)
    return means.T, scores


def solution(mesh):
    return jax.shard_map(
        local,
        mesh=mesh,
        in_specs=(
            P(ALL, None),
            P(ALL, None),
            P(ALL, None, None),
            P(ALL, None),
            P("wide", None),
        ),
        out_specs=(P("narrow", "wide"), P("narrow", "wide")),
        check_vma=False,
    )
```

time: 86.5 us -> 78.6 us (0.909)
  waiting for transfers between devices: 17.7 us -> 8.29 us
  starting transfers between devices: 18.6 us -> 19.9 us
    ppermute x7, waiting for transfers between devices: 16.5 us -> 8.28 us  [the longest x3 8.27 us: local(): lax.ppermute(down, 'wide', Z_DOWN)]
    ppermute x7, starting transfers between devices: 12.1 us -> 15.1 us  [the longest x3 12.3 us: local(): lax.ppermute(down, 'wide', Z_DOWN)]
    pallas_call x2 -> x4, Pallas kernels: 6.65 us -> 9.02 us  [placer(): pl.pallas_call(kernel, out_shape=out_shape, in_specs=[vmem] * len(operand...]
    ppermute x1, starting transfers between devices: 2.16 us -> 0.12 us  [local(): last_partner = lax.ppermute(last, 'wide', CORE_SWAP)]
    pallas_call x1, Pallas kernels: 19.1 us -> 17.1 us  [local(): pl.pallas_call(score_kernel, grid=(K2S // TILE,), out_shape=(jax.ShapeDty...]
    ppermute x1, waiting for transfers between devices: 1.19 us -> 0.01 us  [local(): last_partner = lax.ppermute(last, 'wide', CORE_SWAP)]
  transfers between devices with their start and end apart: 9 -> 9, of which waited for: 6 -> 2; matrix products, arithmetic and copies ran while one was open for 0% -> 0% of each run, Pallas kernels for 5% -> 12%
where the time goes in v3:
time: 78.6 us; the launch traced here: 77.7 us
  Pallas kernels  30 us (38%)
  starting transfers between devices  19.9 us (25%)
  blocking collectives  17.5 us (22%)
  waiting for transfers between devices  8.29 us (11%)
  local copies, waits for them, and re-layouts  1.19 us (2%)
    all_to_all x1, blocking collectives, local(): lax.all_to_all(send, ALL, 0, 0, axis_index_groups=PLANES, tiled=True)  17.5 us
    pallas_call x1, Pallas kernels, local(): pl.pallas_call(score_kernel, grid=(K2S // TILE,), out_shape=(jax.ShapeDty...  17.1 us
    ppermute x3, starting transfers between devices, local(): lax.ppermute(down, 'wide', Z_DOWN)  12.3 us
    pallas_call x4, Pallas kernels, placer(): pl.pallas_call(kernel, out_shape=out_shape, in_specs=[vmem] * len(operand...  9.02 us
    ppermute x3, waiting for transfers between devices, local(): lax.ppermute(down, 'wide', Z_DOWN)  8.27 us
    ppermute x1, starting transfers between devices, local(): partner = lax.ppermute(rounded, 'wide', CORE_SWAP)  4.69 us
    ppermute x1, starting transfers between devices, local(): last = lax.ppermute(down, 'wide', Z_DOWN)  2.75 us
    pallas_call x1, Pallas kernels, local(): pl.pallas_call(pack_kernel, out_shape=jax.ShapeDtypeStruct((SLOTS, HALF +...  2.19 us
  transfers between devices with their start and end apart: 9, of which 2 were waited for; matrix products, arithmetic and copies ran while one was open for 0% of the time, Pallas kernels for 12%

profile of v3, /device:TPU:1, one launch (start us, length us, event | category | flops | bytes accessed | tf_op | source)
XLA Modules:
  0.0 77.7 jit_solution(189463353543797649)
XLA Ops:
  0.6 2.2 %pack.1 = bf16[256,640]{1,0:T(8,128)(2,1)} custom-call(bf16[256,1024]{1,0:T(8,128)(2,1)} %points_ref.1, s32[1,32]{1,0:T(1,128)} %lengths_ref.1, s32[1,32]{1,0:T(1,128)} %bitcast.8, s32[1,32]{1,0:T(1,128)} %rows_ref.1), custom_call_target="tpu_custom_call" | custom-call | tf_op jit(solution)/shard_map/pack/pallas_call | solution.py:192
  2.8 17.5 %all_to_all.11 = bf16[32,8,640]{2,1,0:T(8,128)(2,1)} all-to-all(bf16[32,8,640]{2,1,0:T(8,128)(2,1)} %bitcast.7), channel_id=1, replica_groups={{0,1,2,3,4,5,6,7,8,9,10,11,12,13,14,15,128,129,130,131,132,133,134,135,..., dimensions={0} | all-to-all | bytes 655360 | tf_op jit(solution)/shard_map/all_to_all | solution.py:199
  20.3 1.8 %block.1.refs_0_ = bf16[272,512]{1,0:T(8,128)(2,1)} custom-call(bf16[256,640]{1,0:T(8,128)(2,1)} %bitcast.6), custom_call_target="tpu_custom_call" | custom-call | tf_op jit(solution)/shard_map/block/pallas_call | solution.py:200
  22.1 5.6 %collective-permute-start.3 = (bf16[272,512]{1,0:T(8,128)(2,1)}, bf16[272,512]{1,0:T(8,128)(2,1)S(1)}, u32[]{:S(2)}, u32[]{:S(2)}) collective-permute-start(bf16[272,512]{1,0:T(8,128)(2,1)} %block.1.refs_0_), channel_id=1, source_target_pairs={{0,112},{8,120},{16,0},{24,8},{32,16},{40,24},{48,32},{56,40},{64,... | collective-permute-start | bytes 835592 | tf_op jit(solution)/shard_map/ppermute | solution.py:222
  27.7 0.0 collective-permute-start
  27.7 4.8 %collective-permute-done.3.refs_2_ = bf16[272,512]{1,0:T(8,128)(2,1)S(1)} collective-permute-done((bf16[272,512]{1,0:T(8,128)(2,1)}, bf16[272,512]{1,0:T(8,128)(2,1)S(1)}, u32[]{:S(2)}, u32[]{:S(2)}) %collective-permute-start.3) | collective-permute-done | bytes 278560 | tf_op jit(solution)/shard_map/ppermute | solution.py:222
  32.5 3.3 %collective-permute-start.4 = (bf16[272,512]{1,0:T(8,128)(2,1)S(1)}, bf16[272,512]{1,0:T(8,128)(2,1)S(1)}, u32[]{:S(2)}, u32[]{:S(2)}) collective-permute-start(bf16[272,512]{1,0:T(8,128)(2,1)S(1)} %collective-permute-done.3.refs_2_), channel_id=1, source_target_pairs={{0,112},{8,120},{16,0},{24,8},{32,16},{40,24},{48,32},{56,40},{64,... | collective-permute-start | bytes 835592 | tf_op jit(solution)/shard_map/ppermute | solution.py:222
  35.8 0.0 collective-permute-done.refs_1_
  35.8 0.0 collective-permute-start.1
  35.8 3.5 %collective-permute-done.4.refs_4_ = bf16[272,512]{1,0:T(8,128)(2,1)S(1)} collective-permute-done((bf16[272,512]{1,0:T(8,128)(2,1)S(1)}, bf16[272,512]{1,0:T(8,128)(2,1)S(1)}, u32[]{:S(2)}, u32[]{:S(2)}) %collective-permute-start.4) | collective-permute-done | bytes 278560 | tf_op jit(solution)/shard_map/ppermute | solution.py:222
  39.3 3.5 %collective-permute-start.5 = (bf16[272,512]{1,0:T(8,128)(2,1)S(1)}, bf16[272,512]{1,0:T(8,128)(2,1)S(1)}, u32[]{:S(2)}, u32[]{:S(2)}) collective-permute-start(bf16[272,512]{1,0:T(8,128)(2,1)S(1)} %collective-permute-done.4.refs_4_), channel_id=1, source_target_pairs={{0,112},{8,120},{16,0},{24,8},{32,16},{40,24},{48,32},{56,40},{64,... | collective-permute-start | bytes 835592 | tf_op jit(solution)/shard_map/ppermute | solution.py:222
  42.7 0.0 collective-permute-done.1.refs_3_
  42.7 0.0 collective-permute-start.2
  42.7 0.0 copy-start
  42.7 1.0 %copy-done = bf16[272,512]{1,0:T(8,128)(2,1)S(1)} copy-done((bf16[272,512]{1,0:T(8,128)(2,1)S(1)}, bf16[272,512]{1,0:T(8,128)(2,1)}, u32[]{:S(2)}) %copy-start) | copy-done | bytes 278552
  43.7 3.0 %place_early.1.refs_2_ = f32[1536,512]{1,0:T(8,128)S(1)} custom-call(bf16[272,512]{1,0:T(8,128)(2,1)S(1)} %copy-done, bf16[272,512]{1,0:T(8,128)(2,1)S(1)} %collective-permute-done.refs_1_, bf16[272,512]{1,0:T(8,128)(2,1)S(1)} %collective-permute-done.3.refs_2_, bf16[272,512]{1,0:T(8,128)(2,1)S(1)} %collective-permute-done.1.refs_3_, ...), custom_call_target="tpu_custom_call" | custom-call | flops 3221225472 | bytes 4194304 | tf_op jit(solution)/shard_map/place_early/pallas_call | solution.py:209
  46.7 0.0 copy-start.1
  46.7 0.0 collective-permute-done.5.refs_1_.refs_6_
  46.7 2.7 %collective-permute-start.6 = (bf16[272,512]{1,0:T(8,128)(2,1)S(1)}, bf16[272,512]{1,0:T(8,128)(2,1)S(1)}, u32[]{:S(2)}, u32[]{:S(2)}) collective-permute-start(bf16[272,512]{1,0:T(8,128)(2,1)S(1)} %collective-permute-done.5.refs_1_.refs_6_), channel_id=1, source_target_pairs={{0,112},{8,120},{16,0},{24,8},{32,16},{40,24},{48,32},{56,40},{64,... | collective-permute-start | bytes 835592 | tf_op jit(solution)/shard_map/ppermute | solution.py:224
  49.5 0.0 collective-permute-done.2.refs_0_.refs_5_
  49.5 1.8 %place_late.1 = (f32[1536,512]{1,0:T(8,128)S(1)}, bf16[1536,512]{1,0:T(8,128)(2,1)S(1)}) custom-call(bf16[272,512]{1,0:T(8,128)(2,1)S(1)} %collective-permute-done.2.refs_0_.refs_5_, bf16[272,512]{1,0:T(8,128)(2,1)S(1)} %collective-permute-done.5.refs_1_.refs_6_, f32[1536,512]{1,0:T(8,128)S(1)} %place_early.1.refs_2_), custom_call_target="tpu_custom_call" | custom-call | flops 25769803776 | bytes 4194304 | tf_op jit(solution)/shard_map/place_late/pallas_call | solution.py:209
  51.3 4.7 %collective-permute-start.7 = (bf16[1536,512]{1,0:T(8,128)(2,1)S(1)}, bf16[1536,512]{1,0:T(8,128)(2,1)S(1)}, u32[]{:S(2)}, u32[]{:S(2)}) collective-permute-start(bf16[1536,512]{1,0:T(8,128)(2,1)S(1)} %get-tuple-element.13), channel_id=1, source_target_pairs={{0,8},{8,0},{16,24},{24,16},{32,40},{40,32},{48,56},{56,48},{64,72... | collective-permute-start | bytes 4718600 | tf_op jit(solution)/shard_map/ppermute | solution.py:231
  56.0 0.0 copy-done.1
  56.0 0.0 slice-start
  56.0 2.3 %count.1.tally_ref = f32[1536,16]{1,0:T(8,128)S(1)} custom-call(bf16[272,512]{1,0:T(8,128)(2,1)S(1)} %copy-done.1, bf16[272,512]{1,0:T(8,128)(2,1)S(1)} %collective-permute-done.refs_1_, bf16[272,512]{1,0:T(8,128)(2,1)S(1)} %collective-permute-done.3.refs_2_, bf16[272,512]{1,0:T(8,128)(2,1)S(1)} %collective-permute-done.1.refs_3_, ...), custom_call_target="tpu_custom_call" | custom-call | flops 1048576 | bytes 4194304 | tf_op jit(solution)/shard_map/count/pallas_call | solution.py:209
  58.3 0.0 collective-permute-done.6.last_ref
  58.3 0.1 collective-permute-start.8
  58.4 0.0 slice-start.1
  58.4 1.9 %finish.1 = (bf16[1536,512]{1,0:T(8,128)(2,1)S(1)}, f32[1536,128]{1,0:T(8,128)S(1)}, f32[1536,16]{1,0:T(8,128)S(1)}) custom-call(f32[1536,512]{1,0:T(8,128)S(1)} %get-tuple-element.9.sums_ref, f32[1536,16]{1,0:T(8,128)S(1)} %count.1.tally_ref, bf16[272,512]{1,0:T(8,128)(2,1)S(1)} %collective-permute-done.6.last_ref), custom_call_target="tpu_custom_call" | custom-call | flops 25769803776 | bytes 4194304 | tf_op jit(solution)/shard_map/finish/pallas_call | solution.py:209
  60.3 0.0 collective-permute-done.8.last_partner_ref
  60.4 0.0 collective-permute-done.7.partner_ref
  60.4 0.0 slice-done
  60.4 0.2 slice-done.1
  60.6 17.1 %score.1 = (f32[32,1536]{1,0:T(8,128)}, bf16[1536,4096]{1,0:T(8,128)(2,1)}) custom-call(bf16[1536,512]{1,0:T(8,128)(2,1)S(1)} %get-tuple-element.10.mine_ref, f32[1536,128]{1,0:T(8,128)S(1)} %get-tuple-element.11.squares_ref, f32[1536,16]{1,0:T(8,128)S(1)} %get-tuple-element.12.counts_ref, bf16[1536,512]{1,0:T(8,128)(2,1)S(1)} %collective-permute-done.7.partner_ref, ...), custom_call_target="tpu_custom_call" | custom-call | flops 15032385536 | bytes 25165824 | tf_op jit(solution)/shard_map/score/pallas_call | solution.py:238
  (1 shorter events, 0.0 us)
Async XLA Ops:
  22.1 10.4 %collective-permute-start.3 = (bf16[272,512]{1,0:T(8,128)(2,1)}, bf16[272,512]{1,0:T(8,128)(2,1)S(1)}, u32[]{:S(2)}, u32[]{:S(2)}) collective-permute-start(bf16[272,512]{1,0:T(8,128)(2,1)} %block.1.refs_0_), channel_id=1, source_target_pairs={{0,112},{8,120},{16,0},{24,8},{32,16},{40,24},{48,32},{56,40},{64,... | collective-permute-start | bytes 835592 | tf_op jit(solution)/shard_map/ppermute | solution.py:222
  27.7 8.1 %collective-permute-start = (bf16[272,512]{1,0:T(8,128)(2,1)}, bf16[272,512]{1,0:T(8,128)(2,1)S(1)}, u32[]{:S(2)}, u32[]{:S(2)}) collective-permute-start(bf16[272,512]{1,0:T(8,128)(2,1)} %block.1.refs_0_), channel_id=1, source_target_pairs={{0,16},{8,24},{16,32},{24,40},{32,48},{40,56},{48,64},{56,72},{64,... | collective-permute-start | bytes 835592 | tf_op jit(solution)/shard_map/ppermute | solution.py:222
  32.5 6.8 %collective-permute-start.4 = (bf16[272,512]{1,0:T(8,128)(2,1)S(1)}, bf16[272,512]{1,0:T(8,128)(2,1)S(1)}, u32[]{:S(2)}, u32[]{:S(2)}) collective-permute-start(bf16[272,512]{1,0:T(8,128)(2,1)S(1)} %collective-permute-done.3.refs_2_), channel_id=1, source_target_pairs={{0,112},{8,120},{16,0},{24,8},{32,16},{40,24},{48,32},{56,40},{64,... | collective-permute-start | bytes 835592 | tf_op jit(solution)/shard_map/ppermute | solution.py:222
  35.8 7.0 %collective-permute-start.1 = (bf16[272,512]{1,0:T(8,128)(2,1)S(1)}, bf16[272,512]{1,0:T(8,128)(2,1)S(1)}, u32[]{:S(2)}, u32[]{:S(2)}) collective-permute-start(bf16[272,512]{1,0:T(8,128)(2,1)S(1)} %collective-permute-done.refs_1_), channel_id=1, source_target_pairs={{0,16},{8,24},{16,32},{24,40},{32,48},{40,56},{48,64},{56,72},{64,... | collective-permute-start | bytes 835592 | tf_op jit(solution)/shard_map/ppermute | solution.py:222
  39.3 7.5 %collective-permute-start.5 = (bf16[272,512]{1,0:T(8,128)(2,1)S(1)}, bf16[272,512]{1,0:T(8,128)(2,1)S(1)}, u32[]{:S(2)}, u32[]{:S(2)}) collective-permute-start(bf16[272,512]{1,0:T(8,128)(2,1)S(1)} %collective-permute-done.4.refs_4_), channel_id=1, source_target_pairs={{0,112},{8,120},{16,0},{24,8},{32,16},{40,24},{48,32},{56,40},{64,... | collective-permute-start | bytes 835592 | tf_op jit(solution)/shard_map/ppermute | solution.py:222
  42.7 6.8 %collective-permute-start.2 = (bf16[272,512]{1,0:T(8,128)(2,1)S(1)}, bf16[272,512]{1,0:T(8,128)(2,1)S(1)}, u32[]{:S(2)}, u32[]{:S(2)}) collective-permute-start(bf16[272,512]{1,0:T(8,128)(2,1)S(1)} %collective-permute-done.1.refs_3_), channel_id=1, source_target_pairs={{0,16},{8,24},{16,32},{24,40},{32,48},{40,56},{48,64},{56,72},{64,... | collective-permute-start | bytes 835592 | tf_op jit(solution)/shard_map/ppermute | solution.py:222
  42.7 1.0 %copy-start = (bf16[272,512]{1,0:T(8,128)(2,1)S(1)}, bf16[272,512]{1,0:T(8,128)(2,1)}, u32[]{:S(2)}) copy-start(bf16[272,512]{1,0:T(8,128)(2,1)} %block.1.refs_0_) | copy-start | bytes 835588
  46.7 9.3 %copy-start.1 = (bf16[272,512]{1,0:T(8,128)(2,1)S(1)}, bf16[272,512]{1,0:T(8,128)(2,1)}, u32[]{:S(2)}) copy-start(bf16[272,512]{1,0:T(8,128)(2,1)} %block.1.refs_0_) | copy-start | bytes 835588
  46.7 11.5 %collective-permute-start.6 = (bf16[272,512]{1,0:T(8,128)(2,1)S(1)}, bf16[272,512]{1,0:T(8,128)(2,1)S(1)}, u32[]{:S(2)}, u32[]{:S(2)}) collective-permute-start(bf16[272,512]{1,0:T(8,128)(2,1)S(1)} %collective-permute-done.5.refs_1_.refs_6_), channel_id=1, source_target_pairs={{0,112},{8,120},{16,0},{24,8},{32,16},{40,24},{48,32},{56,40},{64,... | collective-permute-start | bytes 835592 | tf_op jit(solution)/shard_map/ppermute | solution.py:224
  51.3 9.0 %collective-permute-start.7 = (bf16[1536,512]{1,0:T(8,128)(2,1)S(1)}, bf16[1536,512]{1,0:T(8,128)(2,1)S(1)}, u32[]{:S(2)}, u32[]{:S(2)}) collective-permute-start(bf16[1536,512]{1,0:T(8,128)(2,1)S(1)} %get-tuple-element.13), channel_id=1, source_target_pairs={{0,8},{8,0},{16,24},{24,16},{32,40},{40,32},{48,56},{56,48},{64,72... | collective-permute-start | bytes 4718600 | tf_op jit(solution)/shard_map/ppermute | solution.py:231
  56.0 4.3 %slice-start = ((s8[8388608]{0:T(1024)(128)(4,1)}), s8[4194304]{0:T(1024)(128)(4,1)S(1)}, s32[]{:S(2)}) async-start(s8[8388608]{0:T(1024)(128)(4,1)} %bitcast.4), calls=%async_computation.1 | async-start | bytes 8388608
  58.3 2.1 %collective-permute-start.8 = (bf16[272,512]{1,0:T(8,128)(2,1)S(1)}, bf16[272,512]{1,0:T(8,128)(2,1)S(1)}, u32[]{:S(2)}, u32[]{:S(2)}) collective-permute-start(bf16[272,512]{1,0:T(8,128)(2,1)S(1)} %collective-permute-done.6.last_ref), channel_id=1, source_target_pairs={{0,8},{8,0},{16,24},{24,16},{32,40},{40,32},{48,56},{56,48},{64,72... | collective-permute-start | bytes 835592 | tf_op jit(solution)/shard_map/ppermute | solution.py:233
  58.4 2.2 %slice-start.1 = ((s8[8388608]{0:T(1024)(128)(4,1)}), s8[4194304]{0:T(1024)(128)(4,1)S(1)}, s32[]{:S(2)}) async-start(s8[8388608]{0:T(1024)(128)(4,1)} %bitcast.4), calls=%async_computation.2 | async-start | bytes 8388608

commit v4 on v3

--- a/solution.py
+++ b/solution.py
@@ -129,8 +129,7 @@
         counts_ref[chunk(i), :] = count
 
 
-TILE = 512
-PART = 768
+TILE = 1024
 
 
 def finish_kernel(sums_ref, tally_ref, last_ref, mine_ref, squares_ref, counts_ref):
@@ -152,31 +151,29 @@
     w = lax.axis_index("wide")
     core = w % 2
 
-    def score(at):
-        product = lax.dot_general(sums[at, :], two_ref[...], NT, preferred_element_type=F32)
-        scale = jnp.concatenate([inverse[at, :]] * (TILE // LANES), axis=1)
-        scores_ref[at, :] = (product * scale).astype(BF16)
+    def score():
+        product = lax.dot_general(sums[...], two_ref[...], NT, preferred_element_type=F32)
+        scale = jnp.concatenate([inverse[...]] * (TILE // LANES), axis=1)
+        scores_ref[...] = (product * scale).astype(BF16)
 
     @pl.when(pl.program_id(0) == 0)
     def _():
-        for start in range(0, K1S, PART):
-            at = pl.ds(start, PART)
-            hot, _ = hot_rows(start, PART, last_ref)
-            partner = partner_ref[at, :].astype(F32) + jnp.dot(
-                hot, last_partner_ref[:SLOTS, :], preferred_element_type=F32
-            )
-            sums[at, pl.ds(pl.multiple_of(core * HALF, HALF), HALF)] = mine_ref[at, :]
-            sums[at, pl.ds(pl.multiple_of((1 - core) * HALF, HALF), HALF)] = partner.astype(BF16)
-            square = squares_ref[at, :] + jnp.sum(partner * partner, axis=1, keepdims=True)
-            inverse[at, :] = 1.0 / jnp.sqrt(square + 1e-06)
-            lanes = pl.ds(pl.multiple_of(w // 4 * LANES, LANES), LANES)
-            mean = pltpu.roll(sums[at, lanes].astype(F32), (4 - w % 4) % 4 * 32, 1)
-            means_ref[:, at] = (mean / jnp.maximum(counts_ref[at, 2:3], 1.0)).T[:32]
-            score(at)
+        hot, _ = hot_rows(0, K1S, last_ref)
+        partner = partner_ref[...].astype(F32) + jnp.dot(
+            hot, last_partner_ref[:SLOTS, :], preferred_element_type=F32
+        )
+        sums[:, pl.ds(pl.multiple_of(core * HALF, HALF), HALF)] = mine_ref[...]
+        sums[:, pl.ds(pl.multiple_of((1 - core) * HALF, HALF), HALF)] = partner.astype(BF16)
+        square = squares_ref[...] + jnp.sum(partner * partner, axis=1, keepdims=True)
+        inverse[...] = 1.0 / jnp.sqrt(square + 1e-06)
+        lanes = pl.ds(pl.multiple_of(w // 4 * LANES, LANES), LANES)
+        mean = pltpu.roll(sums[:, lanes].astype(F32), (4 - w % 4) % 4 * 32, 1)
+        means_ref[...] = (mean / jnp.maximum(counts_ref[:, 2:3], 1.0)).T[:32]
+        score()
 
     @pl.when(pl.program_id(0) > 0)
     def _():
-        score(pl.ds(0, K1S))
+        score()
 
 
 def whole(shape):
@@ -191,7 +188,7 @@
     vmem = pl.BlockSpec(memory_space=pltpu.VMEM)
     send = pl.pallas_call(
         pack_kernel,
-        out_shape=jax.ShapeDtypeStruct((SLOTS, HALF + LANES), BF16),
+        out_shape=pltpu.VMEM((SLOTS, HALF + LANES), BF16),
         in_specs=[vmem] * 4,
         out_specs=vmem,
         name="pack",
@@ -199,7 +196,7 @@
     received = lax.all_to_all(send, ALL, 0, 0, axis_index_groups=PLANES, tiled=True)
     block = pl.pallas_call(
         block_kernel,
-        out_shape=jax.ShapeDtypeStruct((BLOCK, HALF), BF16),
+        out_shape=pltpu.VMEM((BLOCK, HALF), BF16),
         in_specs=[vmem],
         out_specs=vmem,
         name="block",
@@ -248,7 +245,7 @@
         ],
         out_specs=(whole((32, K1S)), pl.BlockSpec((K1S, TILE), lambda j: (0, j))),
         scratch_shapes=[pltpu.VMEM((K1S, D), BF16), pltpu.VMEM((K1S, LANES), F32)],
-        compiler_params=pltpu.CompilerParams(vmem_limit_bytes=24 << 20),
+        compiler_params=pltpu.CompilerParams(vmem_limit_bytes=32 << 20),
         cost_estimate=cost(14 << 30, 24 << 20),
         name="score",
     )(mine, squares, counts, partner, last, last_partner, level_two)

time: 78.6 us -> 76.4 us (0.972)
  Pallas kernels: 30 us -> 28.1 us
  local copies, waits for them, and re-layouts: 1.19 us -> 0.22 us
  starting transfers between devices: 19.9 us -> 20.8 us
    pallas_call x2, Pallas kernels: 3.94 us -> 2.5 us  [the longest x1 1.46 us: local(): pl.pallas_call(pack_kernel, out_shape=pltpu.VMEM((SLOTS, HALF + LANES), B...]
    unnamed x8 -> x4, local copies, waits for them, and re-layouts: 1.19 us -> 0.22 us
  transfers between devices with their start and end apart: 9 -> 9, of which waited for: 2 -> 3; matrix products, arithmetic and copies ran while one was open for 0% -> 0% of each run, Pallas kernels for 12% -> 12%
where the time goes in v4:
time: 76.4 us; the launch traced here: 75.6 us
  Pallas kernels  28.1 us (37%)
  starting transfers between devices  20.8 us (27%)
  blocking collectives  17.3 us (23%)
  waiting for transfers between devices  8.43 us (11%)
    all_to_all x1, blocking collectives, local(): lax.all_to_all(send, ALL, 0, 0, axis_index_groups=PLANES, tiled=True)  17.3 us
    pallas_call x1, Pallas kernels, local(): pl.pallas_call(score_kernel, grid=(K2S // TILE,), out_shape=(jax.ShapeDty...  16.6 us
    ppermute x3, starting transfers between devices, local(): lax.ppermute(down, 'wide', Z_DOWN)  12.5 us
    pallas_call x4, Pallas kernels, placer(): pl.pallas_call(kernel, out_shape=out_shape, in_specs=[vmem] * len(operand...  9.03 us
    ppermute x3, waiting for transfers between devices, local(): lax.ppermute(down, 'wide', Z_DOWN)  8.42 us
    ppermute x1, starting transfers between devices, local(): partner = lax.ppermute(rounded, 'wide', CORE_SWAP)  4.93 us
    ppermute x1, starting transfers between devices, local(): last = lax.ppermute(down, 'wide', Z_DOWN)  3.12 us
  transfers between devices with their start and end apart: 9, of which 3 were waited for; matrix products, arithmetic and copies ran while one was open for 0% of the time, Pallas kernels for 12%

profile of v4, /device:TPU:1, one launch (start us, length us, event | category | flops | bytes accessed | tf_op | source)
XLA Modules:
  0.0 75.6 jit_solution(12934309089132817496)
XLA Ops:
  0.6 1.5 %pack.1 = bf16[256,640]{1,0:T(8,128)(2,1)S(1)} custom-call(bf16[256,1024]{1,0:T(8,128)(2,1)} %points_ref.1, s32[1,32]{1,0:T(1,128)} %lengths_ref.1, s32[1,32]{1,0:T(1,128)} %bitcast.8, s32[1,32]{1,0:T(1,128)} %rows_ref.1), custom_call_target="tpu_custom_call" | custom-call | tf_op jit(solution)/shard_map/pack/pallas_call | solution.py:189
  2.1 17.3 %all_to_all.11 = bf16[32,8,640]{2,1,0:T(8,128)(2,1)} all-to-all(bf16[32,8,640]{2,1,0:T(8,128)(2,1)S(1)} %bitcast.4), channel_id=1, replica_groups={{0,1,2,3,4,5,6,7,8,9,10,11,12,13,14,15,128,129,130,131,132,133,134,135,..., dimensions={0} | all-to-all | bytes 655360 | tf_op jit(solution)/shard_map/all_to_all | solution.py:196
  19.4 1.0 %block.1.refs_0_ = bf16[272,512]{1,0:T(8,128)(2,1)S(1)} custom-call(bf16[256,640]{1,0:T(8,128)(2,1)} %bitcast.7), custom_call_target="tpu_custom_call" | custom-call | tf_op jit(solution)/shard_map/block/pallas_call | solution.py:197
  20.5 5.6 %collective-permute-start.3 = (bf16[272,512]{1,0:T(8,128)(2,1)S(1)}, bf16[272,512]{1,0:T(8,128)(2,1)S(1)}, u32[]{:S(2)}, u32[]{:S(2)}) collective-permute-start(bf16[272,512]{1,0:T(8,128)(2,1)S(1)} %block.1.refs_0_), channel_id=1, source_target_pairs={{0,112},{8,120},{16,0},{24,8},{32,16},{40,24},{48,32},{56,40},{64,... | collective-permute-start | bytes 835592 | tf_op jit(solution)/shard_map/ppermute | solution.py:219
  26.1 0.0 collective-permute-start
  26.1 4.5 %collective-permute-done.3.refs_2_ = bf16[272,512]{1,0:T(8,128)(2,1)S(1)} collective-permute-done((bf16[272,512]{1,0:T(8,128)(2,1)S(1)}, bf16[272,512]{1,0:T(8,128)(2,1)S(1)}, u32[]{:S(2)}, u32[]{:S(2)}) %collective-permute-start.3) | collective-permute-done | bytes 278560 | tf_op jit(solution)/shard_map/ppermute | solution.py:219
  30.6 3.4 %collective-permute-start.4 = (bf16[272,512]{1,0:T(8,128)(2,1)S(1)}, bf16[272,512]{1,0:T(8,128)(2,1)S(1)}, u32[]{:S(2)}, u32[]{:S(2)}) collective-permute-start(bf16[272,512]{1,0:T(8,128)(2,1)S(1)} %collective-permute-done.3.refs_2_), channel_id=1, source_target_pairs={{0,112},{8,120},{16,0},{24,8},{32,16},{40,24},{48,32},{56,40},{64,... | collective-permute-start | bytes 835592 | tf_op jit(solution)/shard_map/ppermute | solution.py:219
  34.0 0.0 collective-permute-done.refs_1_
  34.0 0.0 collective-permute-start.1
  34.0 3.5 %collective-permute-done.4.refs_4_ = bf16[272,512]{1,0:T(8,128)(2,1)S(1)} collective-permute-done((bf16[272,512]{1,0:T(8,128)(2,1)S(1)}, bf16[272,512]{1,0:T(8,128)(2,1)S(1)}, u32[]{:S(2)}, u32[]{:S(2)}) %collective-permute-start.4) | collective-permute-done | bytes 278560 | tf_op jit(solution)/shard_map/ppermute | solution.py:219
  37.5 3.5 %collective-permute-start.5 = (bf16[272,512]{1,0:T(8,128)(2,1)S(1)}, bf16[272,512]{1,0:T(8,128)(2,1)S(1)}, u32[]{:S(2)}, u32[]{:S(2)}) collective-permute-start(bf16[272,512]{1,0:T(8,128)(2,1)S(1)} %collective-permute-done.4.refs_4_), channel_id=1, source_target_pairs={{0,112},{8,120},{16,0},{24,8},{32,16},{40,24},{48,32},{56,40},{64,... | collective-permute-start | bytes 835592 | tf_op jit(solution)/shard_map/ppermute | solution.py:219
  40.9 0.0 collective-permute-done.1.refs_3_
  40.9 0.0 collective-permute-start.2
  40.9 3.0 %place_early.1.refs_2_ = f32[1536,512]{1,0:T(8,128)S(1)} custom-call(bf16[272,512]{1,0:T(8,128)(2,1)S(1)} %block.1.refs_0_, bf16[272,512]{1,0:T(8,128)(2,1)S(1)} %collective-permute-done.refs_1_, bf16[272,512]{1,0:T(8,128)(2,1)S(1)} %collective-permute-done.3.refs_2_, bf16[272,512]{1,0:T(8,128)(2,1)S(1)} %collective-permute-done.1.refs_3_, ...), custom_call_target="tpu_custom_call" | custom-call | flops 3221225472 | bytes 4194304 | tf_op jit(solution)/shard_map/place_early/pallas_call | solution.py:206
  44.0 0.5 collective-permute-done.5.refs_1_.refs_6_
  44.4 3.1 %collective-permute-start.6 = (bf16[272,512]{1,0:T(8,128)(2,1)S(1)}, bf16[272,512]{1,0:T(8,128)(2,1)S(1)}, u32[]{:S(2)}, u32[]{:S(2)}) collective-permute-start(bf16[272,512]{1,0:T(8,128)(2,1)S(1)} %collective-permute-done.5.refs_1_.refs_6_), channel_id=1, source_target_pairs={{0,112},{8,120},{16,0},{24,8},{32,16},{40,24},{48,32},{56,40},{64,... | collective-permute-start | bytes 835592 | tf_op jit(solution)/shard_map/ppermute | solution.py:221
  47.5 0.0 collective-permute-done.2.refs_0_.refs_5_
  47.5 1.8 %place_late.1 = (f32[1536,512]{1,0:T(8,128)S(1)}, bf16[1536,512]{1,0:T(8,128)(2,1)S(1)}) custom-call(bf16[272,512]{1,0:T(8,128)(2,1)S(1)} %collective-permute-done.2.refs_0_.refs_5_, bf16[272,512]{1,0:T(8,128)(2,1)S(1)} %collective-permute-done.5.refs_1_.refs_6_, f32[1536,512]{1,0:T(8,128)S(1)} %place_early.1.refs_2_), custom_call_target="tpu_custom_call" | custom-call | flops 25769803776 | bytes 4194304 | tf_op jit(solution)/shard_map/place_late/pallas_call | solution.py:206
  49.4 4.9 %collective-permute-start.7 = (bf16[1536,512]{1,0:T(8,128)(2,1)S(1)}, bf16[1536,512]{1,0:T(8,128)(2,1)S(1)}, u32[]{:S(2)}, u32[]{:S(2)}) collective-permute-start(bf16[1536,512]{1,0:T(8,128)(2,1)S(1)} %get-tuple-element.13), channel_id=1, source_target_pairs={{0,8},{8,0},{16,24},{24,16},{32,40},{40,32},{48,56},{56,48},{64,72... | collective-permute-start | bytes 4718600 | tf_op jit(solution)/shard_map/ppermute | solution.py:228
  54.3 0.0 slice-start
  54.3 2.3 %count.1.tally_ref = f32[1536,16]{1,0:T(8,128)S(1)} custom-call(bf16[272,512]{1,0:T(8,128)(2,1)S(1)} %block.1.refs_0_, bf16[272,512]{1,0:T(8,128)(2,1)S(1)} %collective-permute-done.refs_1_, bf16[272,512]{1,0:T(8,128)(2,1)S(1)} %collective-permute-done.3.refs_2_, bf16[272,512]{1,0:T(8,128)(2,1)S(1)} %collective-permute-done.1.refs_3_, ...), custom_call_target="tpu_custom_call" | custom-call | flops 1048576 | bytes 4194304 | tf_op jit(solution)/shard_map/count/pallas_call | solution.py:206
  56.6 0.0 collective-permute-done.6.last_ref
  56.6 0.3 collective-permute-start.8
  56.9 0.0 slice-start.1
  56.9 1.9 %finish.1 = (bf16[1536,512]{1,0:T(8,128)(2,1)S(1)}, f32[1536,128]{1,0:T(8,128)S(1)}, f32[1536,16]{1,0:T(8,128)S(1)}) custom-call(f32[1536,512]{1,0:T(8,128)S(1)} %get-tuple-element.9.sums_ref, f32[1536,16]{1,0:T(8,128)S(1)} %count.1.tally_ref, bf16[272,512]{1,0:T(8,128)(2,1)S(1)} %collective-permute-done.6.last_ref), custom_call_target="tpu_custom_call" | custom-call | flops 25769803776 | bytes 4194304 | tf_op jit(solution)/shard_map/finish/pallas_call | solution.py:206
  58.8 0.0 collective-permute-done.8.last_partner_ref
  58.8 0.0 collective-permute-done.7.partner_ref
  58.8 0.0 slice-done
  58.9 0.2 slice-done.1
  59.1 16.6 %score.1 = (f32[32,1536]{1,0:T(8,128)}, bf16[1536,4096]{1,0:T(8,128)(2,1)}) custom-call(bf16[1536,512]{1,0:T(8,128)(2,1)S(1)} %get-tuple-element.10.mine_ref, f32[1536,128]{1,0:T(8,128)S(1)} %get-tuple-element.11.squares_ref, f32[1536,16]{1,0:T(8,128)S(1)} %get-tuple-element.12.counts_ref, bf16[1536,512]{1,0:T(8,128)(2,1)S(1)} %collective-permute-done.7.partner_ref, ...), custom_call_target="tpu_custom_call" | custom-call | flops 15032385536 | bytes 25165824 | tf_op jit(solution)/shard_map/score/pallas_call | solution.py:235
  (1 shorter events, 0.0 us)
Async XLA Ops:
  20.5 10.1 %collective-permute-start.3 = (bf16[272,512]{1,0:T(8,128)(2,1)S(1)}, bf16[272,512]{1,0:T(8,128)(2,1)S(1)}, u32[]{:S(2)}, u32[]{:S(2)}) collective-permute-start(bf16[272,512]{1,0:T(8,128)(2,1)S(1)} %block.1.refs_0_), channel_id=1, source_target_pairs={{0,112},{8,120},{16,0},{24,8},{32,16},{40,24},{48,32},{56,40},{64,... | collective-permute-start | bytes 835592 | tf_op jit(solution)/shard_map/ppermute | solution.py:219
  26.1 7.9 %collective-permute-start = (bf16[272,512]{1,0:T(8,128)(2,1)S(1)}, bf16[272,512]{1,0:T(8,128)(2,1)S(1)}, u32[]{:S(2)}, u32[]{:S(2)}) collective-permute-start(bf16[272,512]{1,0:T(8,128)(2,1)S(1)} %block.1.refs_0_), channel_id=1, source_target_pairs={{0,16},{8,24},{16,32},{24,40},{32,48},{40,56},{48,64},{56,72},{64,... | collective-permute-start | bytes 835592 | tf_op jit(solution)/shard_map/ppermute | solution.py:219
  30.6 6.9 %collective-permute-start.4 = (bf16[272,512]{1,0:T(8,128)(2,1)S(1)}, bf16[272,512]{1,0:T(8,128)(2,1)S(1)}, u32[]{:S(2)}, u32[]{:S(2)}) collective-permute-start(bf16[272,512]{1,0:T(8,128)(2,1)S(1)} %collective-permute-done.3.refs_2_), channel_id=1, source_target_pairs={{0,112},{8,120},{16,0},{24,8},{32,16},{40,24},{48,32},{56,40},{64,... | collective-permute-start | bytes 835592 | tf_op jit(solution)/shard_map/ppermute | solution.py:219
  34.0 7.0 %collective-permute-start.1 = (bf16[272,512]{1,0:T(8,128)(2,1)S(1)}, bf16[272,512]{1,0:T(8,128)(2,1)S(1)}, u32[]{:S(2)}, u32[]{:S(2)}) collective-permute-start(bf16[272,512]{1,0:T(8,128)(2,1)S(1)} %collective-permute-done.refs_1_), channel_id=1, source_target_pairs={{0,16},{8,24},{16,32},{24,40},{32,48},{40,56},{48,64},{56,72},{64,... | collective-permute-start | bytes 835592 | tf_op jit(solution)/shard_map/ppermute | solution.py:219
  37.5 7.0 %collective-permute-start.5 = (bf16[272,512]{1,0:T(8,128)(2,1)S(1)}, bf16[272,512]{1,0:T(8,128)(2,1)S(1)}, u32[]{:S(2)}, u32[]{:S(2)}) collective-permute-start(bf16[272,512]{1,0:T(8,128)(2,1)S(1)} %collective-permute-done.4.refs_4_), channel_id=1, source_target_pairs={{0,112},{8,120},{16,0},{24,8},{32,16},{40,24},{48,32},{56,40},{64,... | collective-permute-start | bytes 835592 | tf_op jit(solution)/shard_map/ppermute | solution.py:219
  40.9 6.6 %collective-permute-start.2 = (bf16[272,512]{1,0:T(8,128)(2,1)S(1)}, bf16[272,512]{1,0:T(8,128)(2,1)S(1)}, u32[]{:S(2)}, u32[]{:S(2)}) collective-permute-start(bf16[272,512]{1,0:T(8,128)(2,1)S(1)} %collective-permute-done.1.refs_3_), channel_id=1, source_target_pairs={{0,16},{8,24},{16,32},{24,40},{32,48},{40,56},{48,64},{56,72},{64,... | collective-permute-start | bytes 835592 | tf_op jit(solution)/shard_map/ppermute | solution.py:219
  44.4 12.2 %collective-permute-start.6 = (bf16[272,512]{1,0:T(8,128)(2,1)S(1)}, bf16[272,512]{1,0:T(8,128)(2,1)S(1)}, u32[]{:S(2)}, u32[]{:S(2)}) collective-permute-start(bf16[272,512]{1,0:T(8,128)(2,1)S(1)} %collective-permute-done.5.refs_1_.refs_6_), channel_id=1, source_target_pairs={{0,112},{8,120},{16,0},{24,8},{32,16},{40,24},{48,32},{56,40},{64,... | collective-permute-start | bytes 835592 | tf_op jit(solution)/shard_map/ppermute | solution.py:221
  49.4 9.5 %collective-permute-start.7 = (bf16[1536,512]{1,0:T(8,128)(2,1)S(1)}, bf16[1536,512]{1,0:T(8,128)(2,1)S(1)}, u32[]{:S(2)}, u32[]{:S(2)}) collective-permute-start(bf16[1536,512]{1,0:T(8,128)(2,1)S(1)} %get-tuple-element.13), channel_id=1, source_target_pairs={{0,8},{8,0},{16,24},{24,16},{32,40},{40,32},{48,56},{56,48},{64,72... | collective-permute-start | bytes 4718600 | tf_op jit(solution)/shard_map/ppermute | solution.py:228
  54.3 4.5 %slice-start = ((s8[8388608]{0:T(1024)(128)(4,1)}), s8[4194304]{0:T(1024)(128)(4,1)S(1)}, s32[]{:S(2)}) async-start(s8[8388608]{0:T(1024)(128)(4,1)} %bitcast.5), calls=%async_computation.1 | async-start | bytes 8388608
  56.6 2.2 %collective-permute-start.8 = (bf16[272,512]{1,0:T(8,128)(2,1)S(1)}, bf16[272,512]{1,0:T(8,128)(2,1)S(1)}, u32[]{:S(2)}, u32[]{:S(2)}) collective-permute-start(bf16[272,512]{1,0:T(8,128)(2,1)S(1)} %collective-permute-done.6.last_ref), channel_id=1, source_target_pairs={{0,8},{8,0},{16,24},{24,16},{32,40},{40,32},{48,56},{56,48},{64,72... | collective-permute-start | bytes 835592 | tf_op jit(solution)/shard_map/ppermute | solution.py:230
  56.9 2.2 %slice-start.1 = ((s8[8388608]{0:T(1024)(128)(4,1)}), s8[4194304]{0:T(1024)(128)(4,1)S(1)}, s32[]{:S(2)}) async-start(s8[8388608]{0:T(1024)(128)(4,1)} %bitcast.5), calls=%async_computation.2 | async-start | bytes 8388608

commit v5 on v4

--- a/solution.py
+++ b/solution.py
@@ -13,7 +13,7 @@
 CAP = 8
 NARROW = 8
 SLOTS = 256
-BLOCK = 272
+BLOCK = 264
 LANES = 128
 F32 = jnp.float32
 BF16 = jnp.bfloat16
@@ -73,12 +73,12 @@
 def block_kernel(received_ref, out_ref):
     out_ref[:SLOTS, :] = received_ref[:, :HALF]
     tags = received_ref[:, HALF:].astype(F32)
-    turned = jnp.concatenate([tags[:LANES].T[:16], tags[LANES:].T[:16]], axis=1)
+    turned = jnp.concatenate([tags[:LANES].T[:8], tags[LANES:].T[:8]], axis=1)
     out_ref[SLOTS:, :SLOTS] = turned.astype(BF16)
-    out_ref[SLOTS:, SLOTS:] = jnp.zeros((16, HALF - SLOTS), BF16)
-
-
-CHUNK = 256
+    out_ref[SLOTS:, SLOTS:] = jnp.zeros((8, HALF - SLOTS), BF16)
+
+
+CHUNK = 768
 NT = (((1,), (1,)), ((), ()))
 
 
@@ -99,8 +99,15 @@
     return total
 
 
+def fetch_kernel(two_ref, out_ref, token_ref, arrived):
+    copy = pltpu.make_async_copy(two_ref, out_ref, arrived)
+    copy.start()
+    token_ref[...] = jnp.zeros_like(token_ref)
+    copy.wait()
+
+
 def place_early_kernel(*refs):
-    blocks, sums_ref = refs[:-1], refs[-1]
+    blocks, sums_ref = refs[:-2], refs[-1]
 
     @pl.loop(0, K1S // CHUNK)
     def _(i):
@@ -122,7 +129,7 @@
 
     @pl.loop(0, K1S // CHUNK)
     def _(i):
-        count = jnp.zeros((CHUNK, 16), F32)
+        count = jnp.zeros((CHUNK, 8), F32)
         for ref in blocks:
             hot, tags = hot_rows(i * CHUNK, CHUNK, ref)
             count += lax.dot_general(hot, tags, NT, preferred_element_type=F32)
@@ -221,9 +228,19 @@
     last = lax.ppermute(down, "wide", Z_DOWN)
 
     totals, halves, tallies, squares_shape = [
-        jax.ShapeDtypeStruct((K1S, n), t) for n, t in ((HALF, F32), (HALF, BF16), (16, F32), (LANES, F32))
+        jax.ShapeDtypeStruct((K1S, n), t) for n, t in ((HALF, F32), (HALF, BF16), (8, F32), (LANES, F32))
     ]
-    early = placer(place_early_kernel, 3 << 30, totals, *blocks[:5])
+    level_two, token = pl.pallas_call(
+        fetch_kernel,
+        out_shape=(pltpu.VMEM((K2S, D), BF16), jax.ShapeDtypeStruct((8, LANES), F32)),
+        in_specs=[pl.BlockSpec(memory_space=pl.ANY)],
+        out_specs=(vmem, vmem),
+        scratch_shapes=[pltpu.SemaphoreType.DMA],
+        compiler_params=pltpu.CompilerParams(vmem_limit_bytes=12 << 20),
+        cost_estimate=cost(3 << 30, 8 << 20),
+        name="fetch",
+    )(level_two)
+    early = placer(place_early_kernel, 24 << 30, totals, *blocks[:5], token)
     sums, rounded = placer(place_late_kernel, 24 << 30, (totals, halves), up, down, early)
     partner = lax.ppermute(rounded, "wide", CORE_SWAP)
     tally = placer(count_kernel, 1 << 20, tallies, *blocks)

time: 76.4 us -> 74.5 us (0.975)
  local copies, waits for them, and re-layouts: 0.22 us -> 3.38 us
  waiting for transfers between devices: 8.43 us -> 5.46 us
  Pallas kernels: 28.1 us -> 25.9 us
    unnamed x4 -> x2, local copies, waits for them, and re-layouts: 0.22 us -> 3.38 us
    ppermute x3, waiting for transfers between devices: 8.42 us -> 5.33 us  [local(): lax.ppermute(down, 'wide', Z_DOWN)]
    pallas_call x4, Pallas kernels: 9.03 us -> 6.25 us  [placer(): pl.pallas_call(kernel, out_shape=out_shape, in_specs=[vmem] * len(operand...]
  transfers between devices with their start and end apart: 9 -> 9, of which waited for: 3 -> 3; matrix products, arithmetic and copies ran while one was open for 0% -> 0% of each run, Pallas kernels for 12% -> 9%
where the time goes in v5:
time: 74.5 us; the launch traced here: 73.8 us
  Pallas kernels  25.9 us (35%)
  starting transfers between devices  21 us (28%)
  blocking collectives  17.3 us (23%)
  waiting for transfers between devices  5.46 us (7%)
  local copies, waits for them, and re-layouts  3.38 us (5%)
    all_to_all x1, blocking collectives, local(): lax.all_to_all(send, ALL, 0, 0, axis_index_groups=PLANES, tiled=True)  17.3 us
    pallas_call x1, Pallas kernels, local(): pl.pallas_call(score_kernel, grid=(K2S // TILE,), out_shape=(jax.ShapeDty...  16.6 us
    ppermute x3, starting transfers between devices, local(): lax.ppermute(down, 'wide', Z_DOWN)  11.8 us
    pallas_call x4, Pallas kernels, placer(): pl.pallas_call(kernel, out_shape=out_shape, in_specs=[vmem] * len(operand...  6.25 us
    ppermute x3, waiting for transfers between devices, local(): lax.ppermute(down, 'wide', Z_DOWN)  5.33 us
    ppermute x1, starting transfers between devices, local(): partner = lax.ppermute(rounded, 'wide', CORE_SWAP)  5.05 us
    unnamed x2, local copies, waits for them, and re-layouts  3.38 us
    ppermute x1, starting transfers between devices, local(): last = lax.ppermute(down, 'wide', Z_DOWN)  3.12 us
  transfers between devices with their start and end apart: 9, of which 3 were waited for; matrix products, arithmetic and copies ran while one was open for 0% of the time, Pallas kernels for 9%

profile of v5, /device:TPU:1, one launch (start us, length us, event | category | flops | bytes accessed | tf_op | source)
XLA Modules:
  0.0 73.8 jit_solution(14695402304608962843)
XLA Ops:
  0.6 1.5 %pack.1 = bf16[256,640]{1,0:T(8,128)(2,1)S(1)} custom-call(bf16[256,1024]{1,0:T(8,128)(2,1)} %points_ref.1, s32[1,32]{1,0:T(1,128)} %lengths_ref.1, s32[1,32]{1,0:T(1,128)} %bitcast.6, s32[1,32]{1,0:T(1,128)} %rows_ref.1), custom_call_target="tpu_custom_call" | custom-call | tf_op jit(solution)/shard_map/pack/pallas_call | solution.py:196
  2.1 17.3 %all_to_all.11 = bf16[32,8,640]{2,1,0:T(8,128)(2,1)} all-to-all(bf16[32,8,640]{2,1,0:T(8,128)(2,1)S(1)} %bitcast.4), channel_id=1, replica_groups={{0,1,2,3,4,5,6,7,8,9,10,11,12,13,14,15,128,129,130,131,132,133,134,135,..., dimensions={0} | all-to-all | bytes 655360 | tf_op jit(solution)/shard_map/all_to_all | solution.py:203
  19.4 1.0 %block.1.refs_0_ = bf16[264,512]{1,0:T(8,128)(2,1)S(1)} custom-call(bf16[256,640]{1,0:T(8,128)(2,1)} %bitcast.5), custom_call_target="tpu_custom_call" | custom-call | tf_op jit(solution)/shard_map/block/pallas_call | solution.py:204
  20.5 5.6 %collective-permute-start.3 = (bf16[264,512]{1,0:T(8,128)(2,1)S(1)}, bf16[264,512]{1,0:T(8,128)(2,1)S(1)}, u32[]{:S(2)}, u32[]{:S(2)}) collective-permute-start(bf16[264,512]{1,0:T(8,128)(2,1)S(1)} %block.1.refs_0_), channel_id=1, source_target_pairs={{0,112},{8,120},{16,0},{24,8},{32,16},{40,24},{48,32},{56,40},{64,... | collective-permute-start | bytes 811016 | tf_op jit(solution)/shard_map/ppermute | solution.py:226
  26.1 0.0 collective-permute-start
  26.1 4.3 %collective-permute-done.3.refs_2_ = bf16[264,512]{1,0:T(8,128)(2,1)S(1)} collective-permute-done((bf16[264,512]{1,0:T(8,128)(2,1)S(1)}, bf16[264,512]{1,0:T(8,128)(2,1)S(1)}, u32[]{:S(2)}, u32[]{:S(2)}) %collective-permute-start.3) | collective-permute-done | bytes 270368 | tf_op jit(solution)/shard_map/ppermute | solution.py:226
  30.4 3.4 %collective-permute-start.4 = (bf16[264,512]{1,0:T(8,128)(2,1)S(1)}, bf16[264,512]{1,0:T(8,128)(2,1)S(1)}, u32[]{:S(2)}, u32[]{:S(2)}) collective-permute-start(bf16[264,512]{1,0:T(8,128)(2,1)S(1)} %collective-permute-done.3.refs_2_), channel_id=1, source_target_pairs={{0,112},{8,120},{16,0},{24,8},{32,16},{40,24},{48,32},{56,40},{64,... | collective-permute-start | bytes 811016 | tf_op jit(solution)/shard_map/ppermute | solution.py:226
  33.8 0.0 collective-permute-done.refs_1_
  33.8 0.0 collective-permute-start.1
  33.8 0.0 copy-start
  33.8 3.4 %copy-done = bf16[4096,1024]{1,0:T(8,128)(2,1)S(1)} copy-done((bf16[4096,1024]{1,0:T(8,128)(2,1)S(1)}, bf16[4096,1024]{1,0:T(8,128)(2,1)}, u32[]{:S(2)}) %copy-start) | copy-done | bytes 8388632
  37.2 0.6 fetch.1
  37.8 0.0 collective-permute-done.4.refs_4_
  37.8 2.7 %collective-permute-start.5 = (bf16[264,512]{1,0:T(8,128)(2,1)S(1)}, bf16[264,512]{1,0:T(8,128)(2,1)S(1)}, u32[]{:S(2)}, u32[]{:S(2)}) collective-permute-start(bf16[264,512]{1,0:T(8,128)(2,1)S(1)} %collective-permute-done.4.refs_4_), channel_id=1, source_target_pairs={{0,112},{8,120},{16,0},{24,8},{32,16},{40,24},{48,32},{56,40},{64,... | collective-permute-start | bytes 811016 | tf_op jit(solution)/shard_map/ppermute | solution.py:226
  40.5 0.0 collective-permute-done.1.refs_3_
  40.5 0.0 collective-permute-start.2
  40.5 2.4 %place_early.1.refs_2_ = f32[1536,512]{1,0:T(8,128)S(1)} custom-call(bf16[264,512]{1,0:T(8,128)(2,1)S(1)} %block.1.refs_0_, bf16[264,512]{1,0:T(8,128)(2,1)S(1)} %collective-permute-done.refs_1_, bf16[264,512]{1,0:T(8,128)(2,1)S(1)} %collective-permute-done.3.refs_2_, bf16[264,512]{1,0:T(8,128)(2,1)S(1)} %collective-permute-done.1.refs_3_, ...), custom_call_target="tpu_custom_call" | custom-call | flops 25769803776 | bytes 4194304 | tf_op jit(solution)/shard_map/place_early/pallas_call | solution.py:213
  42.9 1.0 %collective-permute-done.5.refs_1_.refs_6_ = bf16[264,512]{1,0:T(8,128)(2,1)S(1)} collective-permute-done((bf16[264,512]{1,0:T(8,128)(2,1)S(1)}, bf16[264,512]{1,0:T(8,128)(2,1)S(1)}, u32[]{:S(2)}, u32[]{:S(2)}) %collective-permute-start.5) | collective-permute-done | bytes 270368 | tf_op jit(solution)/shard_map/ppermute | solution.py:226
  43.9 3.1 %collective-permute-start.6 = (bf16[264,512]{1,0:T(8,128)(2,1)S(1)}, bf16[264,512]{1,0:T(8,128)(2,1)S(1)}, u32[]{:S(2)}, u32[]{:S(2)}) collective-permute-start(bf16[264,512]{1,0:T(8,128)(2,1)S(1)} %collective-permute-done.5.refs_1_.refs_6_), channel_id=1, source_target_pairs={{0,112},{8,120},{16,0},{24,8},{32,16},{40,24},{48,32},{56,40},{64,... | collective-permute-start | bytes 811016 | tf_op jit(solution)/shard_map/ppermute | solution.py:228
  47.0 0.0 collective-permute-done.2.refs_0_.refs_5_
  47.0 1.1 %place_late.1 = (f32[1536,512]{1,0:T(8,128)S(1)}, bf16[1536,512]{1,0:T(8,128)(2,1)S(1)}) custom-call(bf16[264,512]{1,0:T(8,128)(2,1)S(1)} %collective-permute-done.2.refs_0_.refs_5_, bf16[264,512]{1,0:T(8,128)(2,1)S(1)} %collective-permute-done.5.refs_1_.refs_6_, f32[1536,512]{1,0:T(8,128)S(1)} %place_early.1.refs_2_), custom_call_target="tpu_custom_call" | custom-call | flops 25769803776 | bytes 4194304 | tf_op jit(solution)/shard_map/place_late/pallas_call | solution.py:213
  48.2 5.0 %collective-permute-start.7 = (bf16[1536,512]{1,0:T(8,128)(2,1)S(1)}, bf16[1536,512]{1,0:T(8,128)(2,1)S(1)}, u32[]{:S(2)}, u32[]{:S(2)}) collective-permute-start(bf16[1536,512]{1,0:T(8,128)(2,1)S(1)} %get-tuple-element.16), channel_id=1, source_target_pairs={{0,8},{8,0},{16,24},{24,16},{32,40},{40,32},{48,56},{56,48},{64,72... | collective-permute-start | bytes 4718600 | tf_op jit(solution)/shard_map/ppermute | solution.py:245
  53.2 1.7 %count.1.tally_ref = f32[1536,8]{1,0:T(8,128)S(1)} custom-call(bf16[264,512]{1,0:T(8,128)(2,1)S(1)} %block.1.refs_0_, bf16[264,512]{1,0:T(8,128)(2,1)S(1)} %collective-permute-done.refs_1_, bf16[264,512]{1,0:T(8,128)(2,1)S(1)} %collective-permute-done.3.refs_2_, bf16[264,512]{1,0:T(8,128)(2,1)S(1)} %collective-permute-done.1.refs_3_, ...), custom_call_target="tpu_custom_call" | custom-call | flops 1048576 | bytes 4194304 | tf_op jit(solution)/shard_map/count/pallas_call | solution.py:213
  54.9 0.0 collective-permute-done.6.last_ref
  55.0 1.0 %collective-permute-start.8 = (bf16[264,512]{1,0:T(8,128)(2,1)S(1)}, bf16[264,512]{1,0:T(8,128)(2,1)S(1)}, u32[]{:S(2)}, u32[]{:S(2)}) collective-permute-start(bf16[264,512]{1,0:T(8,128)(2,1)S(1)} %collective-permute-done.6.last_ref), channel_id=1, source_target_pairs={{0,8},{8,0},{16,24},{24,16},{32,40},{40,32},{48,56},{56,48},{64,72... | collective-permute-start | bytes 811016 | tf_op jit(solution)/shard_map/ppermute | solution.py:247
  56.0 1.1 %finish.1 = (bf16[1536,512]{1,0:T(8,128)(2,1)S(1)}, f32[1536,128]{1,0:T(8,128)S(1)}, f32[1536,8]{1,0:T(8,128)S(1)}) custom-call(f32[1536,512]{1,0:T(8,128)S(1)} %get-tuple-element.12.sums_ref, f32[1536,8]{1,0:T(8,128)S(1)} %count.1.tally_ref, bf16[264,512]{1,0:T(8,128)(2,1)S(1)} %collective-permute-done.6.last_ref), custom_call_target="tpu_custom_call" | custom-call | flops 25769803776 | bytes 4194304 | tf_op jit(solution)/shard_map/finish/pallas_call | solution.py:213
  57.0 0.1 collective-permute-done.8.last_partner_ref
  57.2 0.0 collective-permute-done.7.partner_ref
  57.2 16.6 %score.1 = (f32[32,1536]{1,0:T(8,128)}, bf16[1536,4096]{1,0:T(8,128)(2,1)}) custom-call(bf16[1536,512]{1,0:T(8,128)(2,1)S(1)} %get-tuple-element.13.mine_ref, f32[1536,128]{1,0:T(8,128)S(1)} %get-tuple-element.14.squares_ref, f32[1536,8]{1,0:T(8,128)S(1)} %get-tuple-element.15.counts_ref, bf16[1536,512]{1,0:T(8,128)(2,1)S(1)} %collective-permute-done.7.partner_ref, ...), custom_call_target="tpu_custom_call" | custom-call | flops 15032385536 | bytes 25165824 | tf_op jit(solution)/shard_map/score/pallas_call | solution.py:252
Async XLA Ops:
  20.5 9.9 %collective-permute-start.3 = (bf16[264,512]{1,0:T(8,128)(2,1)S(1)}, bf16[264,512]{1,0:T(8,128)(2,1)S(1)}, u32[]{:S(2)}, u32[]{:S(2)}) collective-permute-start(bf16[264,512]{1,0:T(8,128)(2,1)S(1)} %block.1.refs_0_), channel_id=1, source_target_pairs={{0,112},{8,120},{16,0},{24,8},{32,16},{40,24},{48,32},{56,40},{64,... | collective-permute-start | bytes 811016 | tf_op jit(solution)/shard_map/ppermute | solution.py:226
  26.1 7.7 %collective-permute-start = (bf16[264,512]{1,0:T(8,128)(2,1)S(1)}, bf16[264,512]{1,0:T(8,128)(2,1)S(1)}, u32[]{:S(2)}, u32[]{:S(2)}) collective-permute-start(bf16[264,512]{1,0:T(8,128)(2,1)S(1)} %block.1.refs_0_), channel_id=1, source_target_pairs={{0,16},{8,24},{16,32},{24,40},{32,48},{40,56},{48,64},{56,72},{64,... | collective-permute-start | bytes 811016 | tf_op jit(solution)/shard_map/ppermute | solution.py:226
  30.4 7.4 %collective-permute-start.4 = (bf16[264,512]{1,0:T(8,128)(2,1)S(1)}, bf16[264,512]{1,0:T(8,128)(2,1)S(1)}, u32[]{:S(2)}, u32[]{:S(2)}) collective-permute-start(bf16[264,512]{1,0:T(8,128)(2,1)S(1)} %collective-permute-done.3.refs_2_), channel_id=1, source_target_pairs={{0,112},{8,120},{16,0},{24,8},{32,16},{40,24},{48,32},{56,40},{64,... | collective-permute-start | bytes 811016 | tf_op jit(solution)/shard_map/ppermute | solution.py:226
  33.8 6.7 %collective-permute-start.1 = (bf16[264,512]{1,0:T(8,128)(2,1)S(1)}, bf16[264,512]{1,0:T(8,128)(2,1)S(1)}, u32[]{:S(2)}, u32[]{:S(2)}) collective-permute-start(bf16[264,512]{1,0:T(8,128)(2,1)S(1)} %collective-permute-done.refs_1_), channel_id=1, source_target_pairs={{0,16},{8,24},{16,32},{24,40},{32,48},{40,56},{48,64},{56,72},{64,... | collective-permute-start | bytes 811016 | tf_op jit(solution)/shard_map/ppermute | solution.py:226
  33.8 3.4 %copy-start = (bf16[4096,1024]{1,0:T(8,128)(2,1)S(1)}, bf16[4096,1024]{1,0:T(8,128)(2,1)}, u32[]{:S(2)}) copy-start(bf16[4096,1024]{1,0:T(8,128)(2,1)} %two_ref.1) | copy-start | bytes 25165828
  37.8 6.2 %collective-permute-start.5 = (bf16[264,512]{1,0:T(8,128)(2,1)S(1)}, bf16[264,512]{1,0:T(8,128)(2,1)S(1)}, u32[]{:S(2)}, u32[]{:S(2)}) collective-permute-start(bf16[264,512]{1,0:T(8,128)(2,1)S(1)} %collective-permute-done.4.refs_4_), channel_id=1, source_target_pairs={{0,112},{8,120},{16,0},{24,8},{32,16},{40,24},{48,32},{56,40},{64,... | collective-permute-start | bytes 811016 | tf_op jit(solution)/shard_map/ppermute | solution.py:226
  40.5 6.5 %collective-permute-start.2 = (bf16[264,512]{1,0:T(8,128)(2,1)S(1)}, bf16[264,512]{1,0:T(8,128)(2,1)S(1)}, u32[]{:S(2)}, u32[]{:S(2)}) collective-permute-start(bf16[264,512]{1,0:T(8,128)(2,1)S(1)} %collective-permute-done.1.refs_3_), channel_id=1, source_target_pairs={{0,16},{8,24},{16,32},{24,40},{32,48},{40,56},{48,64},{56,72},{64,... | collective-permute-start | bytes 811016 | tf_op jit(solution)/shard_map/ppermute | solution.py:226
  43.9 11.0 %collective-permute-start.6 = (bf16[264,512]{1,0:T(8,128)(2,1)S(1)}, bf16[264,512]{1,0:T(8,128)(2,1)S(1)}, u32[]{:S(2)}, u32[]{:S(2)}) collective-permute-start(bf16[264,512]{1,0:T(8,128)(2,1)S(1)} %collective-permute-done.5.refs_1_.refs_6_), channel_id=1, source_target_pairs={{0,112},{8,120},{16,0},{24,8},{32,16},{40,24},{48,32},{56,40},{64,... | collective-permute-start | bytes 811016 | tf_op jit(solution)/shard_map/ppermute | solution.py:228
  48.2 9.0 %collective-permute-start.7 = (bf16[1536,512]{1,0:T(8,128)(2,1)S(1)}, bf16[1536,512]{1,0:T(8,128)(2,1)S(1)}, u32[]{:S(2)}, u32[]{:S(2)}) collective-permute-start(bf16[1536,512]{1,0:T(8,128)(2,1)S(1)} %get-tuple-element.16), channel_id=1, source_target_pairs={{0,8},{8,0},{16,24},{24,16},{32,40},{40,32},{48,56},{56,48},{64,72... | collective-permute-start | bytes 4718600 | tf_op jit(solution)/shard_map/ppermute | solution.py:245
  55.0 2.2 %collective-permute-start.8 = (bf16[264,512]{1,0:T(8,128)(2,1)S(1)}, bf16[264,512]{1,0:T(8,128)(2,1)S(1)}, u32[]{:S(2)}, u32[]{:S(2)}) collective-permute-start(bf16[264,512]{1,0:T(8,128)(2,1)S(1)} %collective-permute-done.6.last_ref), channel_id=1, source_target_pairs={{0,8},{8,0},{16,24},{24,16},{32,40},{40,32},{48,56},{56,48},{64,72... | collective-permute-start | bytes 811016 | tf_op jit(solution)/shard_map/ppermute | solution.py:247

commit v6 on v5

--- a/solution.py
+++ b/solution.py
@@ -153,28 +153,31 @@
 
 def score_kernel(
     mine_ref, squares_ref, counts_ref, partner_ref, last_ref, last_partner_ref, two_ref,
-    means_ref, scores_ref, sums, inverse,
+    means_ref, scores_ref, partner, inverse,
 ):
     w = lax.axis_index("wide")
     core = w % 2
 
     def score():
-        product = lax.dot_general(sums[...], two_ref[...], NT, preferred_element_type=F32)
+        own = pl.ds(pl.multiple_of(core * HALF, HALF), HALF)
+        other = pl.ds(pl.multiple_of((1 - core) * HALF, HALF), HALF)
+        product = lax.dot_general(mine_ref[...], two_ref[:, own], NT, preferred_element_type=F32)
+        product += lax.dot_general(partner[...], two_ref[:, other], NT, preferred_element_type=F32)
         scale = jnp.concatenate([inverse[...]] * (TILE // LANES), axis=1)
         scores_ref[...] = (product * scale).astype(BF16)
 
     @pl.when(pl.program_id(0) == 0)
     def _():
         hot, _ = hot_rows(0, K1S, last_ref)
-        partner = partner_ref[...].astype(F32) + jnp.dot(
+        across = partner_ref[...].astype(F32) + jnp.dot(
             hot, last_partner_ref[:SLOTS, :], preferred_element_type=F32
         )
-        sums[:, pl.ds(pl.multiple_of(core * HALF, HALF), HALF)] = mine_ref[...]
-        sums[:, pl.ds(pl.multiple_of((1 - core) * HALF, HALF), HALF)] = partner.astype(BF16)
-        square = squares_ref[...] + jnp.sum(partner * partner, axis=1, keepdims=True)
+        partner[...] = across.astype(BF16)
+        square = squares_ref[...] + jnp.sum(across * across, axis=1, keepdims=True)
         inverse[...] = 1.0 / jnp.sqrt(square + 1e-06)
-        lanes = pl.ds(pl.multiple_of(w // 4 * LANES, LANES), LANES)
-        mean = pltpu.roll(sums[:, lanes].astype(F32), (4 - w % 4) % 4 * 32, 1)
+        lanes = pl.ds(pl.multiple_of(w % 16 // 4 * LANES, LANES), LANES)
+        mean = jnp.where(w // 16 == core, mine_ref[:, lanes].astype(F32), partner[:, lanes].astype(F32))
+        mean = pltpu.roll(mean, (4 - w % 4) % 4 * 32, 1)
         means_ref[...] = (mean / jnp.maximum(counts_ref[:, 2:3], 1.0)).T[:32]
         score()
 
@@ -261,7 +264,7 @@
             pl.BlockSpec((TILE, D), lambda j: (j, 0)),
         ],
         out_specs=(whole((32, K1S)), pl.BlockSpec((K1S, TILE), lambda j: (0, j))),
-        scratch_shapes=[pltpu.VMEM((K1S, D), BF16), pltpu.VMEM((K1S, LANES), F32)],
+        scratch_shapes=[pltpu.VMEM((K1S, HALF), BF16), pltpu.VMEM((K1S, LANES), F32)],
         compiler_params=pltpu.CompilerParams(vmem_limit_bytes=32 << 20),
         cost_estimate=cost(14 << 30, 24 << 20),
         name="score",

time: 74.5 us -> 74.3 us (level)
  no operation moved by 1% of the time
where the time goes in v6:
time: 74.3 us; the launch traced here: 73.6 us
  Pallas kernels  25.8 us (35%)
  starting transfers between devices  21 us (28%)
  blocking collectives  17.3 us (23%)
  waiting for transfers between devices  5.46 us (7%)
  local copies, waits for them, and re-layouts  3.38 us (5%)
    all_to_all x1, blocking collectives, local(): lax.all_to_all(send, ALL, 0, 0, axis_index_groups=PLANES, tiled=True)  17.3 us
    pallas_call x1, Pallas kernels, local(): pl.pallas_call(score_kernel, grid=(K2S // TILE,), out_shape=(jax.ShapeDty...  16.4 us
    ppermute x3, starting transfers between devices, local(): lax.ppermute(down, 'wide', Z_DOWN)  11.8 us
    pallas_call x4, Pallas kernels, placer(): pl.pallas_call(kernel, out_shape=out_shape, in_specs=[vmem] * len(operand...  6.25 us
    ppermute x3, waiting for transfers between devices, local(): lax.ppermute(down, 'wide', Z_DOWN)  5.33 us
    ppermute x1, starting transfers between devices, local(): partner = lax.ppermute(rounded, 'wide', CORE_SWAP)  5.05 us
    unnamed x2, local copies, waits for them, and re-layouts  3.38 us
    ppermute x1, starting transfers between devices, local(): last = lax.ppermute(down, 'wide', Z_DOWN)  3.12 us
  transfers between devices with their start and end apart: 9, of which 3 were waited for; matrix products, arithmetic and copies ran while one was open for 0% of the time, Pallas kernels for 9%

profile of v6, /device:TPU:1, one launch (start us, length us, event | category | flops | bytes accessed | tf_op | source)
XLA Modules:
  0.0 73.6 jit_solution(11137918123368779761)
XLA Ops:
  0.6 1.5 %pack.1 = bf16[256,640]{1,0:T(8,128)(2,1)S(1)} custom-call(bf16[256,1024]{1,0:T(8,128)(2,1)} %points_ref.1, s32[1,32]{1,0:T(1,128)} %lengths_ref.1, s32[1,32]{1,0:T(1,128)} %bitcast.6, s32[1,32]{1,0:T(1,128)} %rows_ref.1), custom_call_target="tpu_custom_call" | custom-call | tf_op jit(solution)/shard_map/pack/pallas_call | solution.py:199
  2.1 17.3 %all_to_all.11 = bf16[32,8,640]{2,1,0:T(8,128)(2,1)} all-to-all(bf16[32,8,640]{2,1,0:T(8,128)(2,1)S(1)} %bitcast.4), channel_id=1, replica_groups={{0,1,2,3,4,5,6,7,8,9,10,11,12,13,14,15,128,129,130,131,132,133,134,135,..., dimensions={0} | all-to-all | bytes 655360 | tf_op jit(solution)/shard_map/all_to_all | solution.py:206
  19.4 1.0 %block.1.refs_0_ = bf16[264,512]{1,0:T(8,128)(2,1)S(1)} custom-call(bf16[256,640]{1,0:T(8,128)(2,1)} %bitcast.5), custom_call_target="tpu_custom_call" | custom-call | tf_op jit(solution)/shard_map/block/pallas_call | solution.py:207
  20.5 5.6 %collective-permute-start.3 = (bf16[264,512]{1,0:T(8,128)(2,1)S(1)}, bf16[264,512]{1,0:T(8,128)(2,1)S(1)}, u32[]{:S(2)}, u32[]{:S(2)}) collective-permute-start(bf16[264,512]{1,0:T(8,128)(2,1)S(1)} %block.1.refs_0_), channel_id=1, source_target_pairs={{0,112},{8,120},{16,0},{24,8},{32,16},{40,24},{48,32},{56,40},{64,... | collective-permute-start | bytes 811016 | tf_op jit(solution)/shard_map/ppermute | solution.py:229
  26.1 0.0 collective-permute-start
  26.1 4.3 %collective-permute-done.3.refs_2_ = bf16[264,512]{1,0:T(8,128)(2,1)S(1)} collective-permute-done((bf16[264,512]{1,0:T(8,128)(2,1)S(1)}, bf16[264,512]{1,0:T(8,128)(2,1)S(1)}, u32[]{:S(2)}, u32[]{:S(2)}) %collective-permute-start.3) | collective-permute-done | bytes 270368 | tf_op jit(solution)/shard_map/ppermute | solution.py:229
  30.4 3.4 %collective-permute-start.4 = (bf16[264,512]{1,0:T(8,128)(2,1)S(1)}, bf16[264,512]{1,0:T(8,128)(2,1)S(1)}, u32[]{:S(2)}, u32[]{:S(2)}) collective-permute-start(bf16[264,512]{1,0:T(8,128)(2,1)S(1)} %collective-permute-done.3.refs_2_), channel_id=1, source_target_pairs={{0,112},{8,120},{16,0},{24,8},{32,16},{40,24},{48,32},{56,40},{64,... | collective-permute-start | bytes 811016 | tf_op jit(solution)/shard_map/ppermute | solution.py:229
  33.8 0.0 collective-permute-done.refs_1_
  33.8 0.0 collective-permute-start.1
  33.8 0.0 copy-start
  33.8 3.4 %copy-done = bf16[4096,1024]{1,0:T(8,128)(2,1)S(1)} copy-done((bf16[4096,1024]{1,0:T(8,128)(2,1)S(1)}, bf16[4096,1024]{1,0:T(8,128)(2,1)}, u32[]{:S(2)}) %copy-start) | copy-done | bytes 8388632
  37.2 0.6 fetch.1
  37.8 0.0 collective-permute-done.4.refs_4_
  37.8 2.7 %collective-permute-start.5 = (bf16[264,512]{1,0:T(8,128)(2,1)S(1)}, bf16[264,512]{1,0:T(8,128)(2,1)S(1)}, u32[]{:S(2)}, u32[]{:S(2)}) collective-permute-start(bf16[264,512]{1,0:T(8,128)(2,1)S(1)} %collective-permute-done.4.refs_4_), channel_id=1, source_target_pairs={{0,112},{8,120},{16,0},{24,8},{32,16},{40,24},{48,32},{56,40},{64,... | collective-permute-start | bytes 811016 | tf_op jit(solution)/shard_map/ppermute | solution.py:229
  40.5 0.0 collective-permute-done.1.refs_3_
  40.5 0.0 collective-permute-start.2
  40.5 2.4 %place_early.1.refs_2_ = f32[1536,512]{1,0:T(8,128)S(1)} custom-call(bf16[264,512]{1,0:T(8,128)(2,1)S(1)} %block.1.refs_0_, bf16[264,512]{1,0:T(8,128)(2,1)S(1)} %collective-permute-done.refs_1_, bf16[264,512]{1,0:T(8,128)(2,1)S(1)} %collective-permute-done.3.refs_2_, bf16[264,512]{1,0:T(8,128)(2,1)S(1)} %collective-permute-done.1.refs_3_, ...), custom_call_target="tpu_custom_call" | custom-call | flops 25769803776 | bytes 4194304 | tf_op jit(solution)/shard_map/place_early/pallas_call | solution.py:216
  42.9 1.0 %collective-permute-done.5.refs_1_.refs_6_ = bf16[264,512]{1,0:T(8,128)(2,1)S(1)} collective-permute-done((bf16[264,512]{1,0:T(8,128)(2,1)S(1)}, bf16[264,512]{1,0:T(8,128)(2,1)S(1)}, u32[]{:S(2)}, u32[]{:S(2)}) %collective-permute-start.5) | collective-permute-done | bytes 270368 | tf_op jit(solution)/shard_map/ppermute | solution.py:229
  43.9 3.1 %collective-permute-start.6 = (bf16[264,512]{1,0:T(8,128)(2,1)S(1)}, bf16[264,512]{1,0:T(8,128)(2,1)S(1)}, u32[]{:S(2)}, u32[]{:S(2)}) collective-permute-start(bf16[264,512]{1,0:T(8,128)(2,1)S(1)} %collective-permute-done.5.refs_1_.refs_6_), channel_id=1, source_target_pairs={{0,112},{8,120},{16,0},{24,8},{32,16},{40,24},{48,32},{56,40},{64,... | collective-permute-start | bytes 811016 | tf_op jit(solution)/shard_map/ppermute | solution.py:231
  47.0 0.0 collective-permute-done.2.refs_0_.refs_5_
  47.0 1.1 %place_late.1 = (f32[1536,512]{1,0:T(8,128)S(1)}, bf16[1536,512]{1,0:T(8,128)(2,1)S(1)}) custom-call(bf16[264,512]{1,0:T(8,128)(2,1)S(1)} %collective-permute-done.2.refs_0_.refs_5_, bf16[264,512]{1,0:T(8,128)(2,1)S(1)} %collective-permute-done.5.refs_1_.refs_6_, f32[1536,512]{1,0:T(8,128)S(1)} %place_early.1.refs_2_), custom_call_target="tpu_custom_call" | custom-call | flops 25769803776 | bytes 4194304 | tf_op jit(solution)/shard_map/place_late/pallas_call | solution.py:216
  48.2 5.0 %collective-permute-start.7 = (bf16[1536,512]{1,0:T(8,128)(2,1)S(1)}, bf16[1536,512]{1,0:T(8,128)(2,1)S(1)}, u32[]{:S(2)}, u32[]{:S(2)}) collective-permute-start(bf16[1536,512]{1,0:T(8,128)(2,1)S(1)} %get-tuple-element.16), channel_id=1, source_target_pairs={{0,8},{8,0},{16,24},{24,16},{32,40},{40,32},{48,56},{56,48},{64,72... | collective-permute-start | bytes 4718600 | tf_op jit(solution)/shard_map/ppermute | solution.py:248
  53.2 1.7 %count.1.tally_ref = f32[1536,8]{1,0:T(8,128)S(1)} custom-call(bf16[264,512]{1,0:T(8,128)(2,1)S(1)} %block.1.refs_0_, bf16[264,512]{1,0:T(8,128)(2,1)S(1)} %collective-permute-done.refs_1_, bf16[264,512]{1,0:T(8,128)(2,1)S(1)} %collective-permute-done.3.refs_2_, bf16[264,512]{1,0:T(8,128)(2,1)S(1)} %collective-permute-done.1.refs_3_, ...), custom_call_target="tpu_custom_call" | custom-call | flops 1048576 | bytes 4194304 | tf_op jit(solution)/shard_map/count/pallas_call | solution.py:216
  54.9 0.0 collective-permute-done.6.last_ref
  55.0 1.0 %collective-permute-start.8 = (bf16[264,512]{1,0:T(8,128)(2,1)S(1)}, bf16[264,512]{1,0:T(8,128)(2,1)S(1)}, u32[]{:S(2)}, u32[]{:S(2)}) collective-permute-start(bf16[264,512]{1,0:T(8,128)(2,1)S(1)} %collective-permute-done.6.last_ref), channel_id=1, source_target_pairs={{0,8},{8,0},{16,24},{24,16},{32,40},{40,32},{48,56},{56,48},{64,72... | collective-permute-start | bytes 811016 | tf_op jit(solution)/shard_map/ppermute | solution.py:250
  56.0 1.1 %finish.1 = (bf16[1536,512]{1,0:T(8,128)(2,1)S(1)}, f32[1536,128]{1,0:T(8,128)S(1)}, f32[1536,8]{1,0:T(8,128)S(1)}) custom-call(f32[1536,512]{1,0:T(8,128)S(1)} %get-tuple-element.12.sums_ref, f32[1536,8]{1,0:T(8,128)S(1)} %count.1.tally_ref, bf16[264,512]{1,0:T(8,128)(2,1)S(1)} %collective-permute-done.6.last_ref), custom_call_target="tpu_custom_call" | custom-call | flops 25769803776 | bytes 4194304 | tf_op jit(solution)/shard_map/finish/pallas_call | solution.py:216
  57.0 0.1 collective-permute-done.8.last_partner_ref
  57.2 0.0 collective-permute-done.7.partner_ref
  57.2 16.4 %score.1 = (f32[32,1536]{1,0:T(8,128)}, bf16[1536,4096]{1,0:T(8,128)(2,1)}) custom-call(bf16[1536,512]{1,0:T(8,128)(2,1)S(1)} %get-tuple-element.13.mine_ref, f32[1536,128]{1,0:T(8,128)S(1)} %get-tuple-element.14.squares_ref, f32[1536,8]{1,0:T(8,128)S(1)} %get-tuple-element.15.counts_ref, bf16[1536,512]{1,0:T(8,128)(2,1)S(1)} %collective-permute-done.7.partner_ref, ...), custom_call_target="tpu_custom_call" | custom-call | flops 15032385536 | bytes 25165824 | tf_op jit(solution)/shard_map/score/pallas_call | solution.py:255
Async XLA Ops:
  20.5 9.9 %collective-permute-start.3 = (bf16[264,512]{1,0:T(8,128)(2,1)S(1)}, bf16[264,512]{1,0:T(8,128)(2,1)S(1)}, u32[]{:S(2)}, u32[]{:S(2)}) collective-permute-start(bf16[264,512]{1,0:T(8,128)(2,1)S(1)} %block.1.refs_0_), channel_id=1, source_target_pairs={{0,112},{8,120},{16,0},{24,8},{32,16},{40,24},{48,32},{56,40},{64,... | collective-permute-start | bytes 811016 | tf_op jit(solution)/shard_map/ppermute | solution.py:229
  26.1 7.7 %collective-permute-start = (bf16[264,512]{1,0:T(8,128)(2,1)S(1)}, bf16[264,512]{1,0:T(8,128)(2,1)S(1)}, u32[]{:S(2)}, u32[]{:S(2)}) collective-permute-start(bf16[264,512]{1,0:T(8,128)(2,1)S(1)} %block.1.refs_0_), channel_id=1, source_target_pairs={{0,16},{8,24},{16,32},{24,40},{32,48},{40,56},{48,64},{56,72},{64,... | collective-permute-start | bytes 811016 | tf_op jit(solution)/shard_map/ppermute | solution.py:229
  30.4 7.4 %collective-permute-start.4 = (bf16[264,512]{1,0:T(8,128)(2,1)S(1)}, bf16[264,512]{1,0:T(8,128)(2,1)S(1)}, u32[]{:S(2)}, u32[]{:S(2)}) collective-permute-start(bf16[264,512]{1,0:T(8,128)(2,1)S(1)} %collective-permute-done.3.refs_2_), channel_id=1, source_target_pairs={{0,112},{8,120},{16,0},{24,8},{32,16},{40,24},{48,32},{56,40},{64,... | collective-permute-start | bytes 811016 | tf_op jit(solution)/shard_map/ppermute | solution.py:229
  33.8 6.7 %collective-permute-start.1 = (bf16[264,512]{1,0:T(8,128)(2,1)S(1)}, bf16[264,512]{1,0:T(8,128)(2,1)S(1)}, u32[]{:S(2)}, u32[]{:S(2)}) collective-permute-start(bf16[264,512]{1,0:T(8,128)(2,1)S(1)} %collective-permute-done.refs_1_), channel_id=1, source_target_pairs={{0,16},{8,24},{16,32},{24,40},{32,48},{40,56},{48,64},{56,72},{64,... | collective-permute-start | bytes 811016 | tf_op jit(solution)/shard_map/ppermute | solution.py:229
  33.8 3.4 %copy-start = (bf16[4096,1024]{1,0:T(8,128)(2,1)S(1)}, bf16[4096,1024]{1,0:T(8,128)(2,1)}, u32[]{:S(2)}) copy-start(bf16[4096,1024]{1,0:T(8,128)(2,1)} %two_ref.1) | copy-start | bytes 25165828
  37.8 6.2 %collective-permute-start.5 = (bf16[264,512]{1,0:T(8,128)(2,1)S(1)}, bf16[264,512]{1,0:T(8,128)(2,1)S(1)}, u32[]{:S(2)}, u32[]{:S(2)}) collective-permute-start(bf16[264,512]{1,0:T(8,128)(2,1)S(1)} %collective-permute-done.4.refs_4_), channel_id=1, source_target_pairs={{0,112},{8,120},{16,0},{24,8},{32,16},{40,24},{48,32},{56,40},{64,... | collective-permute-start | bytes 811016 | tf_op jit(solution)/shard_map/ppermute | solution.py:229
  40.5 6.5 %collective-permute-start.2 = (bf16[264,512]{1,0:T(8,128)(2,1)S(1)}, bf16[264,512]{1,0:T(8,128)(2,1)S(1)}, u32[]{:S(2)}, u32[]{:S(2)}) collective-permute-start(bf16[264,512]{1,0:T(8,128)(2,1)S(1)} %collective-permute-done.1.refs_3_), channel_id=1, source_target_pairs={{0,16},{8,24},{16,32},{24,40},{32,48},{40,56},{48,64},{56,72},{64,... | collective-permute-start | bytes 811016 | tf_op jit(solution)/shard_map/ppermute | solution.py:229
  43.9 11.0 %collective-permute-start.6 = (bf16[264,512]{1,0:T(8,128)(2,1)S(1)}, bf16[264,512]{1,0:T(8,128)(2,1)S(1)}, u32[]{:S(2)}, u32[]{:S(2)}) collective-permute-start(bf16[264,512]{1,0:T(8,128)(2,1)S(1)} %collective-permute-done.5.refs_1_.refs_6_), channel_id=1, source_target_pairs={{0,112},{8,120},{16,0},{24,8},{32,16},{40,24},{48,32},{56,40},{64,... | collective-permute-start | bytes 811016 | tf_op jit(solution)/shard_map/ppermute | solution.py:231
  48.2 9.0 %collective-permute-start.7 = (bf16[1536,512]{1,0:T(8,128)(2,1)S(1)}, bf16[1536,512]{1,0:T(8,128)(2,1)S(1)}, u32[]{:S(2)}, u32[]{:S(2)}) collective-permute-start(bf16[1536,512]{1,0:T(8,128)(2,1)S(1)} %get-tuple-element.16), channel_id=1, source_target_pairs={{0,8},{8,0},{16,24},{24,16},{32,40},{40,32},{48,56},{56,48},{64,72... | collective-permute-start | bytes 4718600 | tf_op jit(solution)/shard_map/ppermute | solution.py:248
  55.0 2.2 %collective-permute-start.8 = (bf16[264,512]{1,0:T(8,128)(2,1)S(1)}, bf16[264,512]{1,0:T(8,128)(2,1)S(1)}, u32[]{:S(2)}, u32[]{:S(2)}) collective-permute-start(bf16[264,512]{1,0:T(8,128)(2,1)S(1)} %collective-permute-done.6.last_ref), channel_id=1, source_target_pairs={{0,8},{8,0},{16,24},{24,16},{32,40},{40,32},{48,56},{56,48},{64,72... | collective-permute-start | bytes 811016 | tf_op jit(solution)/shard_map/ppermute | solution.py:250

commit v7 on v6

--- a/solution.py
+++ b/solution.py
@@ -139,12 +139,14 @@
 TILE = 1024
 
 
-def finish_kernel(sums_ref, tally_ref, last_ref, mine_ref, squares_ref, counts_ref):
+def finish_kernel(sums_ref, tally_ref, last_ref, mine_ref, squares_ref, counts_ref, hot_ref):
     @pl.loop(0, K1S // CHUNK)
     def _(i):
         at = chunk(i)
         hot, tags = hot_rows(i * CHUNK, CHUNK, last_ref)
-        counts_ref[at, :] = tally_ref[at, :] + lax.dot_general(hot, tags, NT, preferred_element_type=F32)
+        hot_ref[at, :] = hot
+        count = tally_ref[at, :] + lax.dot_general(hot, tags, NT, preferred_element_type=F32)
+        counts_ref[at, :] = jnp.broadcast_to(jnp.maximum(count[:, 2:3], 1.0), (CHUNK, LANES))
         mine = sums_ref[at, :] + jnp.dot(hot, last_ref[:SLOTS, :], preferred_element_type=F32)
         square = jnp.sum(mine * mine, axis=1, keepdims=True)
         mine_ref[at, :] = mine.astype(BF16)
@@ -152,7 +154,7 @@
 
 
 def score_kernel(
-    mine_ref, squares_ref, counts_ref, partner_ref, last_ref, last_partner_ref, two_ref,
+    mine_ref, squares_ref, counts_ref, partner_ref, hot_ref, last_partner_ref, two_ref,
     means_ref, scores_ref, partner, inverse,
 ):
     w = lax.axis_index("wide")
@@ -168,9 +170,8 @@
 
     @pl.when(pl.program_id(0) == 0)
     def _():
-        hot, _ = hot_rows(0, K1S, last_ref)
         across = partner_ref[...].astype(F32) + jnp.dot(
-            hot, last_partner_ref[:SLOTS, :], preferred_element_type=F32
+            hot_ref[...], last_partner_ref[:SLOTS, :], preferred_element_type=F32
         )
         partner[...] = across.astype(BF16)
         square = squares_ref[...] + jnp.sum(across * across, axis=1, keepdims=True)
@@ -178,7 +179,7 @@
         lanes = pl.ds(pl.multiple_of(w % 16 // 4 * LANES, LANES), LANES)
         mean = jnp.where(w // 16 == core, mine_ref[:, lanes].astype(F32), partner[:, lanes].astype(F32))
         mean = pltpu.roll(mean, (4 - w % 4) % 4 * 32, 1)
-        means_ref[...] = (mean / jnp.maximum(counts_ref[:, 2:3], 1.0)).T[:32]
+        means_ref[...] = (mean / counts_ref[...]).T[:32]
         score()
 
     @pl.when(pl.program_id(0) > 0)
@@ -243,13 +244,14 @@
         cost_estimate=cost(3 << 30, 8 << 20),
         name="fetch",
     )(level_two)
+    hot_shape = jax.ShapeDtypeStruct((K1S, SLOTS), BF16)
     early = placer(place_early_kernel, 24 << 30, totals, *blocks[:5], token)
     sums, rounded = placer(place_late_kernel, 24 << 30, (totals, halves), up, down, early)
     partner = lax.ppermute(rounded, "wide", CORE_SWAP)
     tally = placer(count_kernel, 1 << 20, tallies, *blocks)
     last_partner = lax.ppermute(last, "wide", CORE_SWAP)
-    mine, squares, counts = placer(
-        finish_kernel, 24 << 30, (halves, squares_shape, tallies), sums, tally, last
+    mine, squares, counts, hot = placer(
+        finish_kernel, 24 << 30, (halves, squares_shape, squares_shape, hot_shape), sums, tally, last
     )
 
     means, scores = pl.pallas_call(
@@ -268,7 +270,7 @@
         compiler_params=pltpu.CompilerParams(vmem_limit_bytes=32 << 20),
         cost_estimate=cost(14 << 30, 24 << 20),
         name="score",
-    )(mine, squares, counts, partner, last, last_partner, level_two)
+    )(mine, squares, counts, partner, hot, last_partner, level_two)
     return means.T, scores
 
 

time: 74.3 us -> 74.4 us (level)
  no operation moved by 1% of the time
where the time goes in v7:
time: 74.4 us; the launch traced here: 73.7 us
  Pallas kernels  25.8 us (35%)
  starting transfers between devices  21 us (28%)
  blocking collectives  17.3 us (23%)
  waiting for transfers between devices  5.44 us (7%)
  local copies, waits for them, and re-layouts  3.38 us (5%)
    all_to_all x1, blocking collectives, local(): lax.all_to_all(send, ALL, 0, 0, axis_index_groups=PLANES, tiled=True)  17.3 us
    pallas_call x1, Pallas kernels, local(): pl.pallas_call(score_kernel, grid=(K2S // TILE,), out_shape=(jax.ShapeDty...  16.5 us
    ppermute x3, starting transfers between devices, local(): lax.ppermute(down, 'wide', Z_DOWN)  11.8 us
    pallas_call x4, Pallas kernels, placer(): pl.pallas_call(kernel, out_shape=out_shape, in_specs=[vmem] * len(operand...  6.27 us
    ppermute x3, waiting for transfers between devices, local(): lax.ppermute(down, 'wide', Z_DOWN)  5.33 us
    ppermute x1, starting transfers between devices, local(): partner = lax.ppermute(rounded, 'wide', CORE_SWAP)  5.05 us
    unnamed x2, local copies, waits for them, and re-layouts  3.38 us
    ppermute x1, starting transfers between devices, local(): last = lax.ppermute(down, 'wide', Z_DOWN)  3.12 us
  transfers between devices with their start and end apart: 9, of which 3 were waited for; matrix products, arithmetic and copies ran while one was open for 0% of the time, Pallas kernels for 9%

profile of v7, /device:TPU:1, one launch (start us, length us, event | category | flops | bytes accessed | tf_op | source)
XLA Modules:
  0.0 73.7 jit_solution(10897535004696316979)
XLA Ops:
  0.6 1.5 %pack.1 = bf16[256,640]{1,0:T(8,128)(2,1)S(1)} custom-call(bf16[256,1024]{1,0:T(8,128)(2,1)} %points_ref.1, s32[1,32]{1,0:T(1,128)} %lengths_ref.1, s32[1,32]{1,0:T(1,128)} %bitcast.6, s32[1,32]{1,0:T(1,128)} %rows_ref.1), custom_call_target="tpu_custom_call" | custom-call | tf_op jit(solution)/shard_map/pack/pallas_call | solution.py:200
  2.1 17.3 %all_to_all.11 = bf16[32,8,640]{2,1,0:T(8,128)(2,1)} all-to-all(bf16[32,8,640]{2,1,0:T(8,128)(2,1)S(1)} %bitcast.4), channel_id=1, replica_groups={{0,1,2,3,4,5,6,7,8,9,10,11,12,13,14,15,128,129,130,131,132,133,134,135,..., dimensions={0} | all-to-all | bytes 655360 | tf_op jit(solution)/shard_map/all_to_all | solution.py:207
  19.4 1.0 %block.1.refs_0_ = bf16[264,512]{1,0:T(8,128)(2,1)S(1)} custom-call(bf16[256,640]{1,0:T(8,128)(2,1)} %bitcast.5), custom_call_target="tpu_custom_call" | custom-call | tf_op jit(solution)/shard_map/block/pallas_call | solution.py:208
  20.5 5.6 %collective-permute-start.3 = (bf16[264,512]{1,0:T(8,128)(2,1)S(1)}, bf16[264,512]{1,0:T(8,128)(2,1)S(1)}, u32[]{:S(2)}, u32[]{:S(2)}) collective-permute-start(bf16[264,512]{1,0:T(8,128)(2,1)S(1)} %block.1.refs_0_), channel_id=1, source_target_pairs={{0,112},{8,120},{16,0},{24,8},{32,16},{40,24},{48,32},{56,40},{64,... | collective-permute-start | bytes 811016 | tf_op jit(solution)/shard_map/ppermute | solution.py:230
  26.1 0.0 collective-permute-start
  26.1 4.3 %collective-permute-done.3.refs_2_ = bf16[264,512]{1,0:T(8,128)(2,1)S(1)} collective-permute-done((bf16[264,512]{1,0:T(8,128)(2,1)S(1)}, bf16[264,512]{1,0:T(8,128)(2,1)S(1)}, u32[]{:S(2)}, u32[]{:S(2)}) %collective-permute-start.3) | collective-permute-done | bytes 270368 | tf_op jit(solution)/shard_map/ppermute | solution.py:230
  30.4 3.4 %collective-permute-start.4 = (bf16[264,512]{1,0:T(8,128)(2,1)S(1)}, bf16[264,512]{1,0:T(8,128)(2,1)S(1)}, u32[]{:S(2)}, u32[]{:S(2)}) collective-permute-start(bf16[264,512]{1,0:T(8,128)(2,1)S(1)} %collective-permute-done.3.refs_2_), channel_id=1, source_target_pairs={{0,112},{8,120},{16,0},{24,8},{32,16},{40,24},{48,32},{56,40},{64,... | collective-permute-start | bytes 811016 | tf_op jit(solution)/shard_map/ppermute | solution.py:230
  33.8 0.0 collective-permute-done.refs_1_
  33.8 0.0 collective-permute-start.1
  33.8 0.0 copy-start
  33.8 3.4 %copy-done = bf16[4096,1024]{1,0:T(8,128)(2,1)S(1)} copy-done((bf16[4096,1024]{1,0:T(8,128)(2,1)S(1)}, bf16[4096,1024]{1,0:T(8,128)(2,1)}, u32[]{:S(2)}) %copy-start) | copy-done | bytes 8388632
  37.2 0.6 fetch.1
  37.8 0.0 collective-permute-done.4.refs_4_
  37.8 2.7 %collective-permute-start.5 = (bf16[264,512]{1,0:T(8,128)(2,1)S(1)}, bf16[264,512]{1,0:T(8,128)(2,1)S(1)}, u32[]{:S(2)}, u32[]{:S(2)}) collective-permute-start(bf16[264,512]{1,0:T(8,128)(2,1)S(1)} %collective-permute-done.4.refs_4_), channel_id=1, source_target_pairs={{0,112},{8,120},{16,0},{24,8},{32,16},{40,24},{48,32},{56,40},{64,... | collective-permute-start | bytes 811016 | tf_op jit(solution)/shard_map/ppermute | solution.py:230
  40.5 0.0 collective-permute-done.1.refs_3_
  40.5 0.0 collective-permute-start.2
  40.5 2.4 %place_early.1.refs_2_ = f32[1536,512]{1,0:T(8,128)S(1)} custom-call(bf16[264,512]{1,0:T(8,128)(2,1)S(1)} %block.1.refs_0_, bf16[264,512]{1,0:T(8,128)(2,1)S(1)} %collective-permute-done.refs_1_, bf16[264,512]{1,0:T(8,128)(2,1)S(1)} %collective-permute-done.3.refs_2_, bf16[264,512]{1,0:T(8,128)(2,1)S(1)} %collective-permute-done.1.refs_3_, ...), custom_call_target="tpu_custom_call" | custom-call | flops 25769803776 | bytes 4194304 | tf_op jit(solution)/shard_map/place_early/pallas_call | solution.py:217
  42.9 1.0 %collective-permute-done.5.refs_1_.refs_6_ = bf16[264,512]{1,0:T(8,128)(2,1)S(1)} collective-permute-done((bf16[264,512]{1,0:T(8,128)(2,1)S(1)}, bf16[264,512]{1,0:T(8,128)(2,1)S(1)}, u32[]{:S(2)}, u32[]{:S(2)}) %collective-permute-start.5) | collective-permute-done | bytes 270368 | tf_op jit(solution)/shard_map/ppermute | solution.py:230
  43.9 3.1 %collective-permute-start.6 = (bf16[264,512]{1,0:T(8,128)(2,1)S(1)}, bf16[264,512]{1,0:T(8,128)(2,1)S(1)}, u32[]{:S(2)}, u32[]{:S(2)}) collective-permute-start(bf16[264,512]{1,0:T(8,128)(2,1)S(1)} %collective-permute-done.5.refs_1_.refs_6_), channel_id=1, source_target_pairs={{0,112},{8,120},{16,0},{24,8},{32,16},{40,24},{48,32},{56,40},{64,... | collective-permute-start | bytes 811016 | tf_op jit(solution)/shard_map/ppermute | solution.py:232
  47.0 0.0 collective-permute-done.2.refs_0_.refs_5_
  47.0 1.1 %place_late.1 = (f32[1536,512]{1,0:T(8,128)S(1)}, bf16[1536,512]{1,0:T(8,128)(2,1)S(1)}) custom-call(bf16[264,512]{1,0:T(8,128)(2,1)S(1)} %collective-permute-done.2.refs_0_.refs_5_, bf16[264,512]{1,0:T(8,128)(2,1)S(1)} %collective-permute-done.5.refs_1_.refs_6_, f32[1536,512]{1,0:T(8,128)S(1)} %place_early.1.refs_2_), custom_call_target="tpu_custom_call" | custom-call | flops 25769803776 | bytes 4194304 | tf_op jit(solution)/shard_map/place_late/pallas_call | solution.py:217
  48.2 5.0 %collective-permute-start.7 = (bf16[1536,512]{1,0:T(8,128)(2,1)S(1)}, bf16[1536,512]{1,0:T(8,128)(2,1)S(1)}, u32[]{:S(2)}, u32[]{:S(2)}) collective-permute-start(bf16[1536,512]{1,0:T(8,128)(2,1)S(1)} %get-tuple-element.17), channel_id=1, source_target_pairs={{0,8},{8,0},{16,24},{24,16},{32,40},{40,32},{48,56},{56,48},{64,72... | collective-permute-start | bytes 4718600 | tf_op jit(solution)/shard_map/ppermute | solution.py:250
  53.2 1.7 %count.1.tally_ref = f32[1536,8]{1,0:T(8,128)S(1)} custom-call(bf16[264,512]{1,0:T(8,128)(2,1)S(1)} %block.1.refs_0_, bf16[264,512]{1,0:T(8,128)(2,1)S(1)} %collective-permute-done.refs_1_, bf16[264,512]{1,0:T(8,128)(2,1)S(1)} %collective-permute-done.3.refs_2_, bf16[264,512]{1,0:T(8,128)(2,1)S(1)} %collective-permute-done.1.refs_3_, ...), custom_call_target="tpu_custom_call" | custom-call | flops 1048576 | bytes 4194304 | tf_op jit(solution)/shard_map/count/pallas_call | solution.py:217
  54.9 0.0 collective-permute-done.6.last_ref
  55.0 1.0 %collective-permute-start.8 = (bf16[264,512]{1,0:T(8,128)(2,1)S(1)}, bf16[264,512]{1,0:T(8,128)(2,1)S(1)}, u32[]{:S(2)}, u32[]{:S(2)}) collective-permute-start(bf16[264,512]{1,0:T(8,128)(2,1)S(1)} %collective-permute-done.6.last_ref), channel_id=1, source_target_pairs={{0,8},{8,0},{16,24},{24,16},{32,40},{40,32},{48,56},{56,48},{64,72... | collective-permute-start | bytes 811016 | tf_op jit(solution)/shard_map/ppermute | solution.py:252
  56.0 1.1 %finish.1 = (bf16[1536,512]{1,0:T(8,128)(2,1)S(1)}, f32[1536,128]{1,0:T(8,128)S(1)}, f32[1536,128]{1,0:T(8,128)S(1)}, bf16[1536,256]{1,0:T(8,128)(2,1)S(1)}) custom-call(f32[1536,512]{1,0:T(8,128)S(1)} %get-tuple-element.13.sums_ref, f32[1536,8]{1,0:T(8,128)S(1)} %count.1.tally_ref, bf16[264,512]{1,0:T(8,128)(2,1)S(1)} %collective-permute-done.6.last_ref), custom_call_target="tpu_custom_call" | custom-call | flops 25769803776 | bytes 4194304 | tf_op jit(solution)/shard_map/finish/pallas_call | solution.py:217
  57.1 0.1 collective-permute-done.8.last_partner_ref
  57.2 0.0 collective-permute-done.7.partner_ref
  57.2 16.5 %score.1 = (f32[32,1536]{1,0:T(8,128)}, bf16[1536,4096]{1,0:T(8,128)(2,1)}) custom-call(bf16[1536,512]{1,0:T(8,128)(2,1)S(1)} %get-tuple-element.14.mine_ref, f32[1536,128]{1,0:T(8,128)S(1)} %get-tuple-element.15.squares_ref, f32[1536,128]{1,0:T(8,128)S(1)} %get-tuple-element.16.counts_ref, bf16[1536,512]{1,0:T(8,128)(2,1)S(1)} %collective-permute-done.7.partner_ref, ...), custom_call_target="tpu_custom_call" | custom-call | flops 15032385536 | bytes 25165824 | tf_op jit(solution)/shard_map/score/pallas_call | solution.py:257
Async XLA Ops:
  20.5 9.9 %collective-permute-start.3 = (bf16[264,512]{1,0:T(8,128)(2,1)S(1)}, bf16[264,512]{1,0:T(8,128)(2,1)S(1)}, u32[]{:S(2)}, u32[]{:S(2)}) collective-permute-start(bf16[264,512]{1,0:T(8,128)(2,1)S(1)} %block.1.refs_0_), channel_id=1, source_target_pairs={{0,112},{8,120},{16,0},{24,8},{32,16},{40,24},{48,32},{56,40},{64,... | collective-permute-start | bytes 811016 | tf_op jit(solution)/shard_map/ppermute | solution.py:230
  26.1 7.7 %collective-permute-start = (bf16[264,512]{1,0:T(8,128)(2,1)S(1)}, bf16[264,512]{1,0:T(8,128)(2,1)S(1)}, u32[]{:S(2)}, u32[]{:S(2)}) collective-permute-start(bf16[264,512]{1,0:T(8,128)(2,1)S(1)} %block.1.refs_0_), channel_id=1, source_target_pairs={{0,16},{8,24},{16,32},{24,40},{32,48},{40,56},{48,64},{56,72},{64,... | collective-permute-start | bytes 811016 | tf_op jit(solution)/shard_map/ppermute | solution.py:230
  30.4 7.4 %collective-permute-start.4 = (bf16[264,512]{1,0:T(8,128)(2,1)S(1)}, bf16[264,512]{1,0:T(8,128)(2,1)S(1)}, u32[]{:S(2)}, u32[]{:S(2)}) collective-permute-start(bf16[264,512]{1,0:T(8,128)(2,1)S(1)} %collective-permute-done.3.refs_2_), channel_id=1, source_target_pairs={{0,112},{8,120},{16,0},{24,8},{32,16},{40,24},{48,32},{56,40},{64,... | collective-permute-start | bytes 811016 | tf_op jit(solution)/shard_map/ppermute | solution.py:230
  33.8 6.7 %collective-permute-start.1 = (bf16[264,512]{1,0:T(8,128)(2,1)S(1)}, bf16[264,512]{1,0:T(8,128)(2,1)S(1)}, u32[]{:S(2)}, u32[]{:S(2)}) collective-permute-start(bf16[264,512]{1,0:T(8,128)(2,1)S(1)} %collective-permute-done.refs_1_), channel_id=1, source_target_pairs={{0,16},{8,24},{16,32},{24,40},{32,48},{40,56},{48,64},{56,72},{64,... | collective-permute-start | bytes 811016 | tf_op jit(solution)/shard_map/ppermute | solution.py:230
  33.8 3.4 %copy-start = (bf16[4096,1024]{1,0:T(8,128)(2,1)S(1)}, bf16[4096,1024]{1,0:T(8,128)(2,1)}, u32[]{:S(2)}) copy-start(bf16[4096,1024]{1,0:T(8,128)(2,1)} %two_ref.1) | copy-start | bytes 25165828
  37.8 6.2 %collective-permute-start.5 = (bf16[264,512]{1,0:T(8,128)(2,1)S(1)}, bf16[264,512]{1,0:T(8,128)(2,1)S(1)}, u32[]{:S(2)}, u32[]{:S(2)}) collective-permute-start(bf16[264,512]{1,0:T(8,128)(2,1)S(1)} %collective-permute-done.4.refs_4_), channel_id=1, source_target_pairs={{0,112},{8,120},{16,0},{24,8},{32,16},{40,24},{48,32},{56,40},{64,... | collective-permute-start | bytes 811016 | tf_op jit(solution)/shard_map/ppermute | solution.py:230
  40.5 6.5 %collective-permute-start.2 = (bf16[264,512]{1,0:T(8,128)(2,1)S(1)}, bf16[264,512]{1,0:T(8,128)(2,1)S(1)}, u32[]{:S(2)}, u32[]{:S(2)}) collective-permute-start(bf16[264,512]{1,0:T(8,128)(2,1)S(1)} %collective-permute-done.1.refs_3_), channel_id=1, source_target_pairs={{0,16},{8,24},{16,32},{24,40},{32,48},{40,56},{48,64},{56,72},{64,... | collective-permute-start | bytes 811016 | tf_op jit(solution)/shard_map/ppermute | solution.py:230
  43.9 11.0 %collective-permute-start.6 = (bf16[264,512]{1,0:T(8,128)(2,1)S(1)}, bf16[264,512]{1,0:T(8,128)(2,1)S(1)}, u32[]{:S(2)}, u32[]{:S(2)}) collective-permute-start(bf16[264,512]{1,0:T(8,128)(2,1)S(1)} %collective-permute-done.5.refs_1_.refs_6_), channel_id=1, source_target_pairs={{0,112},{8,120},{16,0},{24,8},{32,16},{40,24},{48,32},{56,40},{64,... | collective-permute-start | bytes 811016 | tf_op jit(solution)/shard_map/ppermute | solution.py:232
  48.2 9.0 %collective-permute-start.7 = (bf16[1536,512]{1,0:T(8,128)(2,1)S(1)}, bf16[1536,512]{1,0:T(8,128)(2,1)S(1)}, u32[]{:S(2)}, u32[]{:S(2)}) collective-permute-start(bf16[1536,512]{1,0:T(8,128)(2,1)S(1)} %get-tuple-element.17), channel_id=1, source_target_pairs={{0,8},{8,0},{16,24},{24,16},{32,40},{40,32},{48,56},{56,48},{64,72... | collective-permute-start | bytes 4718600 | tf_op jit(solution)/shard_map/ppermute | solution.py:250
  55.0 2.2 %collective-permute-start.8 = (bf16[264,512]{1,0:T(8,128)(2,1)S(1)}, bf16[264,512]{1,0:T(8,128)(2,1)S(1)}, u32[]{:S(2)}, u32[]{:S(2)}) collective-permute-start(bf16[264,512]{1,0:T(8,128)(2,1)S(1)} %collective-permute-done.6.last_ref), channel_id=1, source_target_pairs={{0,8},{8,0},{16,24},{24,16},{32,40},{40,32},{48,56},{56,48},{64,72... | collective-permute-start | bytes 811016 | tf_op jit(solution)/shard_map/ppermute | solution.py:252
